TPU v7x, 32 devices: a whole 2x2x4 slice. The times are simulated.
32 devices in a mesh: row: 4 (over y, x), col: 8 (over z, core).
Axes of the slice: x: 2, y: 2, z: 4, core: 2. Of those that a mesh axis runs over, the one named last changes fastest.
Arguments:
- segments: float32 [12288, 512], P(('row', 'col')), may hold values from -60 to 60
- exclusion: int32 [1], replicated, may hold values from 1 to 12
Outputs:
- profile: float32 [2, 12288], P(None, ('row', 'col'))
All inputs are finite; a program needn't handle non-finite values.
Results may differ from a plain program's by a relative error of at most 0.0005.
Values may be sent and summed in bfloat16 or wider, within the bound.
A program may use at most 192 MiB of HBM per device.

v0:
```python
import math

import jax
import jax.numpy as jnp
from jax import lax
from jax.sharding import PartitionSpec as P


def statistics(segments):
    seg_len = segments.shape[1]
    average = jnp.mean(segments, axis=1)
    centered = segments - average[:, None]
    spread_inv = lax.rsqrt(jnp.mean(centered * centered, axis=1) + 1e-05) * (
        1.0 / math.sqrt(seg_len)
    )
    return (average, spread_inv)


def normalize(samples, average, spread_inv):
    return ((samples - average[:, None]) * spread_inv[:, None]).astype(jnp.bfloat16)


def tile_minima(row_data, row_pos, upper_rows, lower_rows, col_data, col_pos, exclude):
    products = lax.dot_general(
        row_data, col_data, (((1,), (1,)), ((), ())), preferred_element_type=jnp.float32
    )
    apart = 1.0 - products
    offset_by = col_pos[None, :] - row_pos[:, None]
    upper_mask = (offset_by > exclude) & upper_rows[:, None]
    lower_mask = (offset_by < -exclude) & lower_rows[:, None]
    upper_dist = jnp.where(upper_mask, apart, 4.0)
    lower_dist = jnp.where(lower_mask, apart, 4.0)
    row_part = jnp.stack([jnp.min(lower_dist, axis=1), jnp.min(upper_dist, axis=1)])
    col_part = jnp.stack([jnp.min(upper_dist, axis=0), jnp.min(lower_dist, axis=0)])
    return (row_part, col_part)


def shards(segments, exclusion):
    seg_rows = segments.shape[0]
    n_row = lax.axis_size("row")
    n_col = lax.axis_size("col")
    my_row = lax.axis_index("row")
    my_col = lax.axis_index("col")
    exclude = exclusion[0]
    average, spread_inv = statistics(segments)
    col_index = jnp.arange(n_row * seg_rows, dtype=jnp.int32)
    col_pos = (col_index // seg_rows * n_col + my_col) * seg_rows + col_index % seg_rows
    initial = (
        jnp.full((2, n_col * seg_rows), 4.0, jnp.float32),
        jnp.full((2, n_row * seg_rows), 4.0, jnp.float32),
    )
    col_raw, col_average, col_spread = (
        lax.all_gather(segments, "row", axis=0, tiled=True),
        lax.all_gather(average, "row", axis=0, tiled=True),
        lax.all_gather(spread_inv, "row", axis=0, tiled=True),
    )
    columns = normalize(col_raw, col_average, col_spread)
    totals = initial
    normed_rows = normalize(
        lax.all_gather(segments, "col", axis=0, tiled=True),
        lax.all_gather(average, "col", axis=0, tiled=True),
        lax.all_gather(spread_inv, "col", axis=0, tiled=True),
    )
    offset = jnp.int32(0)
    count = normed_rows.shape[0]
    for step_idx in range(count // seg_rows):
        row_data = normed_rows[step_idx * seg_rows : (step_idx + 1) * seg_rows]
        visit_offset = offset + step_idx * seg_rows
        visit_row_min, visit_col_min = totals
        visit_count = row_data.shape[0]
        panel_idx = visit_offset + jnp.arange(visit_count, dtype=jnp.int32)
        row_pos = my_row * n_col * seg_rows + panel_idx
        part_row, part_col = tile_minima(
            row_data, row_pos, row_pos >= 0, row_pos < 0, columns, col_pos, exclude
        )
        visit_col_min = jnp.minimum(visit_col_min, part_col)
        previous = lax.dynamic_slice_in_dim(visit_row_min, visit_offset, visit_count, 1)
        visit_row_min = lax.dynamic_update_slice_in_dim(
            visit_row_min, jnp.minimum(previous, part_row), visit_offset, 1
        )
        totals = (visit_row_min, visit_col_min)
    row_min, col_min = totals
    from_rows = lax.all_to_all(
        row_min.reshape(2, n_col, seg_rows), "col", split_axis=1, concat_axis=1, tiled=True
    )
    from_cols = lax.all_to_all(
        col_min.reshape(2, n_row, seg_rows), "row", split_axis=1, concat_axis=1, tiled=True
    )
    return jnp.minimum(jnp.min(from_rows, axis=1), jnp.min(from_cols, axis=1))


def solution(mesh):
    return jax.shard_map(
        shards,
        mesh=mesh,
        in_specs=(P(("row", "col"), None), P()),
        out_specs=P(None, ("row", "col")),
        check_vma=False,
    )
```

profile of v0, /device:TPU:0, one launch (start us, length us, event | category | flops | bytes accessed | tf_op | source)
XLA Modules:
  0.0 180.3 jit_solution(909898295768622947)
XLA Ops:
  6.5 0.0 copy-start
  6.5 0.0 all-gather.9.cloned.1.call-start
  6.5 0.7 all-gather.9.cloned.1.call-update
  7.3 0.0 all-gather.7.cloned.1.call-start
  7.3 0.7 all-gather.7.cloned.1.call-update
  8.0 1.3 reduce_sum.18
  9.3 0.0 copy-done
  9.3 0.2 multiply_reduce_fusion
  9.6 9.5 %all-gather.3 = f32[4,1,384]{2,1,0:T(1,128)S(1)} all-gather(f32[1,1,384]{2,1,0:T(1,128)S(1)} %reshape.154), channel_id=1, replica_groups=mesh['row'=4,'col'=8] {'row'}, dimensions={0}, use_global_device_ids=true | all-gather | bytes 7680 | tf_op jit(solution)/shard_map/all_gather | solution.py:55
  19.1 8.1 %all-gather.2 = f32[4,1,384]{2,1,0:T(1,128)S(1)} all-gather(f32[1,1,384]{2,1,0:T(1,128)S(1)} %reshape.152), channel_id=1, replica_groups=mesh['row'=4,'col'=8] {'row'}, dimensions={0}, use_global_device_ids=true | all-gather | bytes 7680 | tf_op jit(solution)/shard_map/all_gather | solution.py:54
  27.9 12.9 %all-gather.1 = f32[8,1,384]{2,1,0:T(1,128)S(1)} all-gather(f32[1,1,384]{2,1,0:T(1,128)S(1)} %reshape.154), channel_id=1, replica_groups=mesh['row'=4,'col'=8] {'col'}, dimensions={0}, use_global_device_ids=true | all-gather | bytes 13824 | tf_op jit(solution)/shard_map/all_gather | solution.py:62
  40.8 12.7 %all-gather = f32[8,1,384]{2,1,0:T(1,128)S(1)} all-gather(f32[1,1,384]{2,1,0:T(1,128)S(1)} %reshape.152), channel_id=1, replica_groups=mesh['row'=4,'col'=8] {'col'}, dimensions={0}, use_global_device_ids=true | all-gather | bytes 13824 | tf_op jit(solution)/shard_map/all_gather | solution.py:61
  53.7 2.3 %all-gather.9.cloned.1.call-done = f32[1536,512]{1,0:T(8,128)} async-done(((f32[384,512]{1,0:T(8,128)}), f32[1536,512]{1,0:T(8,128)}) %all-gather.9.cloned.1.call-update) | async-done | bytes 3145744 | tf_op jit(solution)/shard_map/all_gather | solution.py:53
  55.9 3.5 %multiply_convert_fusion.1 = bf16[1536,512]{1,0:T(8,128)(2,1)} fusion(f32[1536,512]{1,0:T(8,128)} %all-gather.9.cloned.1.call-done, f32[1536]{0:T(1024)S(1)} %reshape.159, f32[1536]{0:T(1024)S(1)} %reshape.157), kind=kLoop, calls=%fused_computation.17 | loop fusion | flops 2359296 | bytes 4730880 | tf_op jit(solution)/shard_map/convert_element_type | solution.py:20
  59.5 62.9 %all-gather.7.cloned.1.call-done = f32[3072,512]{1,0:T(8,128)} async-done(((f32[384,512]{1,0:T(8,128)}), f32[3072,512]{1,0:T(8,128)}) %all-gather.7.cloned.1.call-update) | async-done | bytes 6291472 | tf_op jit(solution)/shard_map/all_gather | solution.py:60
  122.4 0.0 copy-start.1
  122.4 3.8 %multiply_convert_fusion = bf16[3072,512]{1,0:T(8,128)(2,1)S(1)} fusion(f32[3072,512]{1,0:T(8,128)} %all-gather.7.cloned.1.call-done, f32[3072]{0:T(1024)S(1)} %bitcast.15, f32[3072]{0:T(1024)S(1)} %bitcast.16), kind=kLoop, calls=%fused_computation | loop fusion | flops 4718592 | bytes 9461760 | tf_op jit(solution)/shard_map/convert_element_type | solution.py:20
  126.2 0.0 copy-done.1
  126.2 0.8 convolution_subtract_fusion.3
  127.0 0.8 convolution_subtract_fusion.4
  127.8 0.8 convolution_subtract_fusion.5
  128.6 2.2 %convolution_subtract_fusion.1 = f32[384,1536]{1,0:T(8,128)} fusion(bf16[1536,512]{1,0:T(8,128)(2,1)S(1)} %copy-done.1, bf16[3072,512]{1,0:T(8,128)(2,1)S(1)} %multiply_convert_fusion), kind=kOutput, calls=%fused_computation.19 | convolution fusion | flops 604569600 | bytes 4325376 | tf_op jit(solution)/shard_map/dot_general | solution.py:24
  130.8 2.3 %convolution_subtract_fusion.2 = f32[384,1536]{1,0:T(8,128)} fusion(bf16[1536,512]{1,0:T(8,128)(2,1)S(1)} %copy-done.1, bf16[3072,512]{1,0:T(8,128)(2,1)S(1)} %multiply_convert_fusion), kind=kOutput, calls=%fused_computation.20 | convolution fusion | flops 604569600 | bytes 4325376 | tf_op jit(solution)/shard_map/dot_general | solution.py:24
  133.1 2.2 %convolution_subtract_fusion = f32[384,1536]{1,0:T(8,128)} fusion(bf16[1536,512]{1,0:T(8,128)(2,1)S(1)} %copy-done.1, bf16[3072,512]{1,0:T(8,128)(2,1)S(1)} %multiply_convert_fusion), kind=kOutput, calls=%fused_computation.18 | convolution fusion | flops 604569600 | bytes 4325376 | tf_op jit(solution)/shard_map/dot_general | solution.py:24
  135.3 6.3 %fusion.56 = (f32[1536]{0:T(1024)S(1)}, f32[384]{0:T(512)S(1)}, f32[384]{0:T(512)S(1)}, f32[1536]{0:T(1024)S(1)}, f32[1536]{0:T(1024)S(1)}, /*index=5*/f32[384]{...) fusion(s32[384]{0:T(512)S(1)} %get-tuple-element.83, ...), kind=kOutput, calls=%fused_computation.82 | convolution fusion | flops 630506496 | bytes 9125896 | tf_op jit(solution)/shard_map/dot_general | solution.py:24
  141.8 8.7 %fusion.60 = (f32[1536]{0:T(1024)S(1)}, f32[384]{0:T(512)S(1)}, f32[384]{0:T(512)S(1)}, f32[1536]{0:T(1024)S(1)}, f32[1536]{0:T(1024)S(1)}, /*index=5*/f32[384]{...) fusion(s32[]{:T(128)} %bitcast.14, ...), kind=kOutput, calls=%fused_computation.86 | convolution fusion | flops 630506496 | bytes 9125896 | tf_op jit(solution)/shard_map/dot_general | solution.py:24
  150.6 0.7 fusion.81
  151.3 3.7 %all-to-all-start.1 = ((f32[2,4,384]{2,0,1:T(2,128)}), f32[2,4,384]{2,0,1:T(2,128)S(1)}, u32[]{:S(2)}, u32[]{:S(2)}) async-start(f32[2,4,384]{2,0,1:T(2,128)} %fusion.81), calls=%async_computation.1 | async-start | bytes 24576 | tf_op jit(solution)/shard_map/all_to_all | solution.py:86
  155.1 0.6 dynamic_update_slice.24
  155.7 0.6 fusion.95
  156.3 1.3 fusion.94
  157.6 1.3 fusion.93
  158.8 1.3 fusion.92
  160.1 1.3 fusion.91
  161.4 1.3 fusion.90
  162.6 1.3 fusion.89
  163.9 0.0 all-to-all-done.1
  163.9 3.3 %all-to-all-start = ((f32[2,8,384]{2,0,1:T(2,128)}), f32[2,8,384]{2,0,1:T(2,128)S(1)}, u32[]{:S(2)}, u32[]{:S(2)}) async-start(f32[2,8,384]{2,0,1:T(2,128)} %bitcast.3), calls=%async_computation | async-start | bytes 49152 | tf_op jit(solution)/shard_map/all_to_all | solution.py:83
  167.3 5.6 %all-to-all-done = f32[2,8,384]{2,0,1:T(2,128)S(1)} async-done(((f32[2,8,384]{2,0,1:T(2,128)}), f32[2,8,384]{2,0,1:T(2,128)S(1)}, u32[]{:S(2)}, u32[]{:S(2)}) %all-to-all-start) | async-done | bytes 24608 | tf_op jit(solution)/shard_map/all_to_all | solution.py:83
  172.9 0.6 min.66
  (56 shorter events, 0.5 us)
Async XLA Ops:
  6.5 2.8 %copy-start = (f32[384,512]{1,0:T(8,128)S(1)}, f32[384,512]{1,0:T(8,128)}, u32[]{:S(2)}) copy-start(f32[384,512]{1,0:T(8,128)} %param.2) | copy-start | bytes 2359300
  6.5 49.4 %all-gather.9.cloned.1.call-start = ((), (), s32[]{:S(2)}) async-start(), calls=%async_computation.3 | async-start | bytes 3932160 | tf_op jit(solution)/shard_map/all_gather | solution.py:53
  7.3 115.1 %all-gather.7.cloned.1.call-start = ((), (), s32[]{:S(2)}) async-start(), calls=%async_computation.2 | async-start | bytes 7077888 | tf_op jit(solution)/shard_map/all_gather | solution.py:60
  122.4 3.8 %copy-start.1 = (bf16[1536,512]{1,0:T(8,128)(2,1)S(1)}, bf16[1536,512]{1,0:T(8,128)(2,1)}, u32[]{:S(2)}) copy-start(bf16[1536,512]{1,0:T(8,128)(2,1)} %multiply_convert_fusion.1) | copy-start | bytes 4718596
  151.3 12.6 %all-to-all-start.1 = ((f32[2,4,384]{2,0,1:T(2,128)}), f32[2,4,384]{2,0,1:T(2,128)S(1)}, u32[]{:S(2)}, u32[]{:S(2)}) async-start(f32[2,4,384]{2,0,1:T(2,128)} %fusion.81), calls=%async_computation.1 | async-start | bytes 24576 | tf_op jit(solution)/shard_map/all_to_all | solution.py:86
  163.9 9.0 %all-to-all-start = ((f32[2,8,384]{2,0,1:T(2,128)}), f32[2,8,384]{2,0,1:T(2,128)S(1)}, u32[]{:S(2)}, u32[]{:S(2)}) async-start(f32[2,8,384]{2,0,1:T(2,128)} %bitcast.3), calls=%async_computation | async-start | bytes 49152 | tf_op jit(solution)/shard_map/all_to_all | solution.py:83
Sparse Core Ops, SparseCore 0:
  9.2 46.6 all-gather.8
  57.6 64.7 all-gather.6
where the time goes:
time: 181 us; the launch traced here: 180 us
  waiting for transfers between devices  72.2 us (40%)
  blocking collectives  43.2 us (24%)
  matrix products  24.1 us (13%)
  other arithmetic  18.5 us (10%)
  between operations  14.4 us (8%)
  starting transfers between devices  7.03 us (4%)
    all_gather x1, waiting for transfers between devices, shards(): lax.all_gather(segments, 'col', axis=0, tiled=True)  62.9 us
    dot_general x8, matrix products, tile_minima(): lax.dot_general(row_data, col_data, (((1,), (1,)), ((), ())), preferred_e...  24.1 us
    all_gather x1, blocking collectives, shards(): lax.all_gather(spread_inv, 'col', axis=0, tiled=True)  12.9 us
    all_gather x1, blocking collectives, shards(): lax.all_gather(average, 'col', axis=0, tiled=True)  12.7 us
    all_gather x1, blocking collectives, shards(): lax.all_gather(spread_inv, 'row', axis=0, tiled=True)  9.52 us
    dynamic_update_slice x7, other arithmetic, shards(): lax.dynamic_update_slice_in_dim(visit_row_min, jnp.minimum(previous, part...  8.18 us
    all_gather x1, blocking collectives, shards(): lax.all_gather(average, 'row', axis=0, tiled=True)  8.06 us
    convert_element_type x2, other arithmetic, normalize(): ((samples - average[:, None]) * spread_inv[:, None]).astype(jnp.bfloat16)  7.33 us
  transfers between devices with their start and end apart: 4, of which 3 were waited for; matrix products, arithmetic and copies ran while one was open for 8% of the time, Pallas kernels for 0%

commit v1 on v0

v1 whole, which is shorter than its diff:
```python
import functools
import math

import jax
import jax.numpy as jnp
from jax import lax
from jax.experimental import pallas as pl
from jax.experimental.pallas import tpu as pltpu
from jax.sharding import PartitionSpec as P

MESH = pl.DeviceIdType.MESH
NONE = -3.0
MARGIN = 128
CHUNKS = 4
TILE = 256


def kernel(
    n_row, n_col, seg_ref, exclusion_ref, out_ref, plane, line, row_acc, col_acc,
    col_out, col_in, row_out, row_in, plane_recv, line_recv, col_recv, row_recv,
    data_send, line_send, col_send, row_send,
):
    rows, seg_len = seg_ref.shape
    n_z = n_col // 2
    step = rows // CHUNKS
    my_l = lax.axis_index("row")
    my_col = lax.axis_index("col")
    my_z = my_col // 2
    my_c = my_col % 2
    exclude = exclusion_ref[0]
    shifts = list(range(1, (n_z - 1) // 2 + 1))
    tie = n_z // 2 if n_z % 2 == 0 else 0
    if tie:
        shifts.append(tie)
    upper = my_z // max(tie, 1)
    tie_recv = (my_z % max(tie, 1) + upper) % 2 == 1
    tie_send = (my_z % max(tie, 1) + upper) % 2 == 0
    forwarding = n_row == 4
    if forwarding:
        x_peer = my_l + 1 - 2 * (my_l % 2)
        y_peer = my_l + 2 - 4 * (my_l // 2)
        peers = [x_peer, y_peer, 3 - my_l]
    else:
        peers = [(my_l + o) % n_row for o in range(1, n_row)]

    def device(l, z, c):
        return (l, z * 2 + c)

    barrier = pltpu.get_barrier_semaphore()
    greeted = [device(my_l, my_z, 1 - my_c)]
    for l in peers:
        greeted += [device(l, my_z, my_c), device(l, my_z, 1 - my_c)]
    for d in range(1, n_z):
        greeted.append(device(my_l, (my_z + d) % n_z, my_c))
    for target in greeted:
        pl.semaphore_signal(barrier, inc=1, device_id=target, device_id_type=MESH)

    def normalise(k):
        samples = seg_ref[pl.ds(k * step, step), :]
        average = jnp.mean(samples, axis=1, keepdims=True)
        centered = samples - average
        spread_inv = lax.rsqrt(jnp.mean(centered * centered, axis=1, keepdims=True) + 1e-05) * (
            1.0 / math.sqrt(seg_len)
        )
        plane[my_l, pl.ds(pl.multiple_of(my_c * rows + k * step, 16), step), :] = (
            centered * spread_inv
        ).astype(jnp.bfloat16)

    def part(l, c, k):
        return plane.at[l, pl.ds(pl.multiple_of(c * rows + k * step, 16), step), :]

    started = []

    def send_part(l, c, k, target):
        idx = len(started)
        copy = pltpu.make_async_remote_copy(
            src_ref=part(l, c, k), dst_ref=part(l, c, k), send_sem=data_send.at[idx],
            recv_sem=plane_recv.at[l, c, k], device_id=target, device_id_type=MESH,
        )
        copy.start()
        started.append(copy)

    def await_part(l, c, k):
        pltpu.make_async_remote_copy(
            src_ref=part(l, c, k), dst_ref=part(l, c, k), send_sem=data_send.at[0],
            recv_sem=plane_recv.at[l, c, k], device_id=greeted[0], device_id_type=MESH,
        ).wait_recv()

    def line_copy(i, k):
        d = shifts[i]
        return pltpu.make_async_remote_copy(
            src_ref=part(my_l, my_c, k), dst_ref=line.at[i, pl.ds(k * step, step), :],
            send_sem=line_send.at[i, k], recv_sem=line_recv.at[i, k],
            device_id=device(my_l, (my_z + n_z - d) % n_z, my_c), device_id_type=MESH,
        )

    normalise(0)
    pl.semaphore_wait(barrier, len(greeted))
    sibling = greeted[0]
    for k in range(CHUNKS):
        if k:
            normalise(k)
        for i, d in enumerate(shifts):
            if d != tie:
                line_copy(i, k).start()
        for l in peers[:2] if forwarding else peers:
            send_part(my_l, my_c, k, device(l, my_z, my_c))
        send_part(my_l, my_c, k, sibling)
    if tie:
        @pl.when(tie_send)
        def _():
            for k in range(CHUNKS):
                line_copy(len(shifts) - 1, k).start()

    row_acc[...] = jnp.full(row_acc.shape, NONE, jnp.float32)
    col_acc[...] = jnp.full(col_acc.shape, NONE, jnp.float32)

    def tiles(lhs, slot, z_from, first, count, l, width, with_cols):
        row_start = ((my_l * n_z + z_from) * 2 + my_c) * rows + first
        span = pl.ds(first, count)

        def update_rows(side, values):
            best = values[:, :128]
            for g in range(1, width // 128):
                best = jnp.maximum(best, values[:, g * 128 : (g + 1) * 128])
            row_acc[slot, side, span, :] = jnp.maximum(row_acc[slot, side, span, :], best)

        def update_cols(side, cols, values):
            if with_cols:
                best = jnp.max(values.reshape(count // 8, 8, width), axis=0)
                col_acc[l, side, :, cols] = jnp.maximum(col_acc[l, side, :, cols], best)

        def body(t, carry):
            begin = pl.multiple_of(t * width, width)
            cols = pl.ds(begin, width)
            col_start = (l * n_z + my_z) * 2 * rows + begin

            def products():
                return lax.dot_general(
                    lhs(span), plane[l, cols, :], (((1,), (1,)), ((), ())),
                    preferred_element_type=jnp.float32,
                )

            near = (col_start < row_start + count + MARGIN) & (
                row_start < col_start + width + MARGIN
            )

            @pl.when(near)
            def _():
                p = products()
                apart = (col_start - row_start) + (
                    lax.broadcasted_iota(jnp.int32, (count, width), 1)
                    - lax.broadcasted_iota(jnp.int32, (count, width), 0)
                )
                later = jnp.where(apart > exclude, p, NONE)
                earlier = jnp.where(apart < -exclude, p, NONE)
                update_rows(1, later)
                update_rows(0, earlier)
                update_cols(0, cols, later)
                update_cols(1, cols, earlier)

            @pl.when(jnp.logical_not(near))
            def _():
                p = products()
                side = (col_start > row_start).astype(jnp.int32)
                update_rows(side, p)
                update_cols(1 - side, cols, p)

            return carry

        lax.fori_loop(0, 2 * rows // width, body, 0)

    def own_with(l):
        tiles(lambda span: part_rows(span), 0, my_z, 0, rows, l, TILE, False)

    def part_rows(span):
        return plane[my_l, pl.ds(pl.multiple_of(my_c * rows + span.start, 16), span.size), :]

    def line_with(i, l, first, count, width):
        tiles(
            lambda span: line[i, span, :], i + 1, (my_z + shifts[i]) % n_z,
            first, count, l, width, True,
        )

    def await_line(i, k):
        line_copy(i, k).wait_recv()

    for k in range(CHUNKS):
        await_part(my_l, 1 - my_c, k)
    own_with(my_l)
    if forwarding:
        for k in range(CHUNKS):
            await_part(x_peer, my_c, k)
            if k < CHUNKS // 2:
                send_part(x_peer, my_c, k, device(y_peer, my_z, my_c))
            send_part(x_peer, my_c, k, sibling)
            await_part(y_peer, my_c, k)
            if k >= CHUNKS // 2:
                send_part(y_peer, my_c, k, device(x_peer, my_z, my_c))
            send_part(y_peer, my_c, k, sibling)
        early, late = peers[:2], peers[2:]
    else:
        early, late = peers, []
        for l in early:
            for k in range(CHUNKS):
                await_part(l, my_c, k)
                send_part(l, my_c, k, sibling)
    for l in early:
        for k in range(CHUNKS):
            await_part(l, 1 - my_c, k)
        own_with(l)
    order = [k // 2 + (k % 2) * (CHUNKS // 2) for k in range(CHUNKS)]
    for l in late:
        for k in order[: CHUNKS // 2]:
            await_part(l, my_c, k)
            send_part(l, my_c, k, sibling)
    whole = [i for i, d in enumerate(shifts) if d != tie]
    for i in whole:
        for k in range(CHUNKS):
            await_line(i, k)
        for l in [my_l] + early:
            line_with(i, l, 0, rows, TILE)
    for l in late:
        for k in order[CHUNKS // 2 :]:
            await_part(l, my_c, k)
            send_part(l, my_c, k, sibling)
        for k in range(CHUNKS):
            await_part(l, 1 - my_c, k)
        own_with(l)
        for i in whole:
            line_with(i, l, 0, rows, TILE)

    def send_rows(i):
        for side in range(2):
            row_out[i, side : side + 1, :] = jnp.max(
                row_acc[i + 1, side].T, axis=0, keepdims=True
            )
        row_copy(i).start()

    def row_copy(i):
        return pltpu.make_async_remote_copy(
            src_ref=row_out.at[i], dst_ref=row_in.at[i], send_sem=row_send.at[i],
            recv_sem=row_recv.at[i],
            device_id=device(my_l, (my_z + shifts[i]) % n_z, my_c), device_id_type=MESH,
        )

    for i in whole:
        send_rows(i)
    if tie:
        @pl.when(tie_recv)
        def _():
            i = len(shifts) - 1
            for k in range(CHUNKS):
                await_line(i, k)

                def each(o, carry):
                    line_with(i, o, k * step, step, 2 * rows)
                    return carry

                lax.fori_loop(0, n_row, each, 0)
            send_rows(i)

    def col_copy(l, c):
        return pltpu.make_async_remote_copy(
            src_ref=col_out.at[l, c], dst_ref=col_in.at[my_l, my_c],
            send_sem=col_send.at[l, c], recv_sem=col_recv.at[my_l, my_c],
            device_id=device(l, my_z, c), device_id_type=MESH,
        )

    def await_col(l, c):
        pltpu.make_async_remote_copy(
            src_ref=col_out.at[l, c], dst_ref=col_in.at[l, c],
            send_sem=col_send.at[l, c], recv_sem=col_recv.at[l, c],
            device_id=device(l, my_z, c), device_id_type=MESH,
        ).wait_recv()

    remote = [(l, c) for l in peers for c in (my_c, 1 - my_c)] + [(my_l, 1 - my_c)]
    for l in peers + [my_l]:
        for side in range(2):
            best = jnp.max(col_acc[l, side], axis=0, keepdims=True)
            for c in range(2):
                col_out[l, c, side : side + 1, :] = best[:, c * rows : (c + 1) * rows]
        for c in (1 - my_c,) if l is my_l else (my_c, 1 - my_c):
            col_copy(l, c).start()

    best = jnp.concatenate(
        [jnp.max(row_acc[0, side].T, axis=0, keepdims=True) for side in range(2)], axis=0
    )
    best = jnp.maximum(best, col_out[my_l, my_c])
    for l, c in remote:
        await_col(l, c)
        best = jnp.maximum(best, col_in[l, c])
    for i in whole:
        row_copy(i).wait_recv()
        best = jnp.maximum(best, row_in[i])
    out_ref[...] = 1.0 - best
    if tie:
        @pl.when(tie_send)
        def _():
            i = len(shifts) - 1
            row_copy(i).wait_recv()
            out_ref[...] = jnp.minimum(out_ref[...], 1.0 - row_in[i])

    for copy in started:
        copy.wait_send()
    for i in whole:
        for k in range(CHUNKS):
            line_copy(i, k).wait_send()
        row_copy(i).wait_send()
    for l, c in remote:
        col_copy(l, c).wait_send()
    if tie:
        @pl.when(tie_send)
        def _():
            for k in range(CHUNKS):
                line_copy(len(shifts) - 1, k).wait_send()

        @pl.when(tie_recv)
        def _():
            row_copy(len(shifts) - 1).wait_send()


def shards(segments, exclusion):
    rows, seg_len = segments.shape
    n_row = lax.axis_size("row")
    n_col = lax.axis_size("col")
    n_z = n_col // 2
    slots = n_z // 2
    sends = CHUNKS * (3 * n_row)
    dma = pltpu.SemaphoreType.DMA
    return pl.pallas_call(
        functools.partial(kernel, n_row, n_col),
        out_shape=jax.ShapeDtypeStruct((2, rows), jnp.float32),
        in_specs=[
            pl.BlockSpec(memory_space=pltpu.VMEM),
            pl.BlockSpec(memory_space=pltpu.SMEM),
        ],
        out_specs=pl.BlockSpec(memory_space=pltpu.VMEM),
        scratch_shapes=[
            pltpu.VMEM((n_row, 2 * rows, seg_len), jnp.bfloat16),
            pltpu.VMEM((slots, rows, seg_len), jnp.bfloat16),
            pltpu.VMEM((slots + 1, 2, rows, 128), jnp.float32),
            pltpu.VMEM((n_row, 2, 8, 2 * rows), jnp.float32),
            pltpu.VMEM((n_row, 2, 2, rows), jnp.float32),
            pltpu.VMEM((n_row, 2, 2, rows), jnp.float32),
            pltpu.VMEM((slots, 2, rows), jnp.float32),
            pltpu.VMEM((slots, 2, rows), jnp.float32),
            dma((n_row, 2, CHUNKS)),
            dma((slots, CHUNKS)),
            dma((n_row, 2)),
            dma((slots,)),
            dma((sends,)),
            dma((slots, CHUNKS)),
            dma((n_row, 2)),
            dma((slots,)),
        ],
        compiler_params=pltpu.CompilerParams(
            collective_id=0, has_side_effects=True, vmem_limit_bytes=48 * 1024 * 1024
        ),
        cost_estimate=pl.CostEstimate(
            flops=2 * rows * 2 * rows * n_row * seg_len * (slots + 1),
            bytes_accessed=rows * seg_len * 4,
            transcendentals=0,
        ),
    )(segments, exclusion)


def solution(mesh):
    return jax.shard_map(
        shards,
        mesh=mesh,
        in_specs=(P(("row", "col"), None), P()),
        out_specs=P(None, ("row", "col")),
        check_vma=False,
    )
```

time: 181 us -> 37.2 us (0.21)
  waiting for transfers between devices: 72.2 us -> 0 us
  blocking collectives: 43.2 us -> 0 us
  Pallas kernels: 0 us -> 34.6 us
  matrix products: 24.1 us -> 0 us
  other arithmetic: 18.5 us -> 0 us
  between operations: 14.4 us -> 0.67 us
  starting transfers between devices: 7.03 us -> 0 us
    all_gather x2 -> x0, waiting for transfers between devices: 65.2 us -> none  [the longest x1 62.9 us: shards(): lax.all_gather(segments, 'col', axis=0, tiled=True)]
    all_gather x4 -> x0, blocking collectives: 43.2 us -> none  [the longest x1 12.9 us: shards(): lax.all_gather(spread_inv, 'col', axis=0, tiled=True)]
    pallas_call x0 -> x1, Pallas kernels: none -> 34.6 us  [shards(): pl.pallas_call(functools.partial(kernel, n_row, n_col), out_shape=jax.Sha...]
    dot_general x8 -> x0, matrix products: 24.1 us -> none  [tile_minima(): lax.dot_general(row_data, col_data, (((1,), (1,)), ((), ())), preferred_e...]
    dynamic_update_slice x7 -> x0, other arithmetic: 8.18 us -> none  [shards(): lax.dynamic_update_slice_in_dim(visit_row_min, jnp.minimum(previous, part...]
    convert_element_type x2 -> x0, other arithmetic: 7.33 us -> none  [normalize(): ((samples - average[:, None]) * spread_inv[:, None]).astype(jnp.bfloat16)]
    all_to_all x2 -> x0, starting transfers between devices: 6.99 us -> none  [the longest x1 3.66 us: shards(): lax.all_to_all(col_min.reshape(2, n_row, seg_rows), 'row', split_axis=1,...]
    all_to_all x2 -> x0, waiting for transfers between devices: 5.61 us -> none  [the longest x1 5.61 us: shards(): lax.all_to_all(row_min.reshape(2, n_col, seg_rows), 'col', split_axis=1,...]
  transfers between devices with their start and end apart: 4 -> 0, of which waited for: 3 -> 0; matrix products, arithmetic and copies ran while one was open for 8% -> 0% of each run, Pallas kernels for 0% -> 0%
where the time goes in v1:
time: 37.2 us; the launch traced here: 37 us
  Pallas kernels  34.6 us (93%)
  local copies, waits for them, and re-layouts  1.71 us (5%)
  between operations  0.67 us (2%)
    pallas_call x1, Pallas kernels, shards(): pl.pallas_call(functools.partial(kernel, n_row, n_col), out_shape=jax.Sha...  34.6 us
    unnamed x3, local copies, waits for them, and re-layouts  1.71 us

profile of v1, /device:TPU:0, one launch (start us, length us, event | category | flops | bytes accessed | tf_op | source)
XLA Modules:
  0.0 37.0 jit_solution(7853775629943588156)
XLA Ops:
  0.7 0.0 copy-start
  0.7 1.1 %copy-done = f32[384,512]{1,0:T(8,128)S(1)} copy-done((f32[384,512]{1,0:T(8,128)S(1)}, f32[384,512]{1,0:T(8,128)}, u32[]{:S(2)}) %copy-start) | copy-done | bytes 786456
  1.8 34.6 %shard_map.28 = f32[2,384]{1,0:T(2,128)S(1)} custom-call(f32[384,512]{1,0:T(8,128)S(1)} %copy-done, s32[1]{0:T(128)S(6)} %copy.4.exclusion_ref), custom_call_target="tpu_custom_call" | custom-call | flops 3623878656 | bytes 786432 | tf_op jit(solution)/shard_map/pallas_call | solution.py:331
  36.4 0.6 %copy.5 = f32[2,384]{1,0:T(2,128)} copy(f32[2,384]{1,0:T(2,128)S(1)} %shard_map.28) | data formatting | bytes 6144
Async XLA Ops:
  0.7 1.1 %copy-start = (f32[384,512]{1,0:T(8,128)S(1)}, f32[384,512]{1,0:T(8,128)}, u32[]{:S(2)}) copy-start(f32[384,512]{1,0:T(8,128)} %seg_ref.1) | copy-start | bytes 2359300

commit v2 on v1

--- a/solution.py
+++ b/solution.py
@@ -10,13 +10,12 @@
 
 MESH = pl.DeviceIdType.MESH
 NONE = -3.0
-MARGIN = 128
 CHUNKS = 4
 TILE = 256
 
 
 def kernel(
-    n_row, n_col, seg_ref, exclusion_ref, out_ref, plane, line, row_acc, col_acc,
+    n_row, n_col, seg_hbm, exclusion_ref, out_ref, seg_ref, in_sem, plane, line, row_acc, col_acc,
     col_out, col_in, row_out, row_in, plane_recv, line_recv, col_recv, row_recv,
     data_send, line_send, col_send, row_send,
 ):
@@ -27,7 +26,14 @@
     my_col = lax.axis_index("col")
     my_z = my_col // 2
     my_c = my_col % 2
-    exclude = exclusion_ref[0]
+    loads = [
+        pltpu.make_async_copy(
+            seg_hbm.at[pl.ds(k * step, step), :], seg_ref.at[pl.ds(k * step, step), :], in_sem.at[k]
+        )
+        for k in range(CHUNKS)
+    ]
+    for load in loads:
+        load.start()
     shifts = list(range(1, (n_z - 1) // 2 + 1))
     tie = n_z // 2 if n_z % 2 == 0 else 0
     if tie:
@@ -56,6 +62,7 @@
         pl.semaphore_signal(barrier, inc=1, device_id=target, device_id_type=MESH)
 
     def normalise(k):
+        loads[k].wait()
         samples = seg_ref[pl.ds(k * step, step), :]
         average = jnp.mean(samples, axis=1, keepdims=True)
         centered = samples - average
@@ -115,7 +122,7 @@
     row_acc[...] = jnp.full(row_acc.shape, NONE, jnp.float32)
     col_acc[...] = jnp.full(col_acc.shape, NONE, jnp.float32)
 
-    def tiles(lhs, slot, z_from, first, count, l, width, with_cols):
+    def block(lhs, slot, z_from, first, count, l, width, near, with_cols):
         row_start = ((my_l * n_z + z_from) * 2 + my_c) * rows + first
         span = pl.ds(first, count)
 
@@ -130,25 +137,17 @@
                 best = jnp.max(values.reshape(count // 8, 8, width), axis=0)
                 col_acc[l, side, :, cols] = jnp.maximum(col_acc[l, side, :, cols], best)
 
-        def body(t, carry):
-            begin = pl.multiple_of(t * width, width)
-            cols = pl.ds(begin, width)
-            col_start = (l * n_z + my_z) * 2 * rows + begin
-
-            def products():
-                return lax.dot_general(
-                    lhs(span), plane[l, cols, :], (((1,), (1,)), ((), ())),
-                    preferred_element_type=jnp.float32,
-                )
-
-            near = (col_start < row_start + count + MARGIN) & (
-                row_start < col_start + width + MARGIN
+        def products(cols):
+            return lax.dot_general(
+                lhs(span), plane[l, cols, :], (((1,), (1,)), ((), ())),
+                preferred_element_type=jnp.float32,
             )
 
-            @pl.when(near)
-            def _():
-                p = products()
-                apart = (col_start - row_start) + (
+        def masked():
+            for begin in range(0, 2 * rows, width):
+                cols = pl.ds(begin, width)
+                p = products(cols)
+                apart = ((l * n_z + my_z) * 2 * rows + begin - row_start) + (
                     lax.broadcasted_iota(jnp.int32, (count, width), 1)
                     - lax.broadcasted_iota(jnp.int32, (count, width), 0)
                 )
@@ -159,32 +158,41 @@
                 update_cols(0, cols, later)
                 update_cols(1, cols, earlier)
 
-            @pl.when(jnp.logical_not(near))
-            def _():
-                p = products()
-                side = (col_start > row_start).astype(jnp.int32)
+        def plain():
+            side = ((l * n_z + my_z) * 2 * rows > row_start).astype(jnp.int32)
+            for begin in range(0, 2 * rows, width):
+                cols = pl.ds(begin, width)
+                p = products(cols)
                 update_rows(side, p)
                 update_cols(1 - side, cols, p)
 
-            return carry
-
-        lax.fori_loop(0, 2 * rows // width, body, 0)
+        if isinstance(near, bool):
+            masked() if near else plain()
+        else:
+            pl.when(near)(masked)
+            pl.when(jnp.logical_not(near))(plain)
 
     def own_with(l):
-        tiles(lambda span: part_rows(span), 0, my_z, 0, rows, l, TILE, False)
+        block(part_rows, 0, my_z, 0, rows, l, TILE, n_z == 1 or l is my_l, False)
 
     def part_rows(span):
         return plane[my_l, pl.ds(pl.multiple_of(my_c * rows + span.start, 16), span.size), :]
 
     def line_with(i, l, first, count, width):
-        tiles(
-            lambda span: line[i, span, :], i + 1, (my_z + shifts[i]) % n_z,
-            first, count, l, width, True,
+        d = shifts[i]
+        near = False
+        if min(d, n_z - d) == 1:
+            gap = (l - my_l) * n_z + my_z - (my_z + d) % n_z
+            near = (gap >= -1) & (gap <= 1)
+        block(
+            lambda span: line[i, span, :], i + 1, (my_z + d) % n_z,
+            first, count, l, width, near, True,
         )
 
     def await_line(i, k):
         line_copy(i, k).wait_recv()
 
+    exclude = exclusion_ref[0]
     for k in range(CHUNKS):
         await_part(my_l, 1 - my_c, k)
     own_with(my_l)
@@ -246,6 +254,9 @@
 
     for i in whole:
         send_rows(i)
+    own_best = jnp.concatenate(
+        [jnp.max(row_acc[0, side].T, axis=0, keepdims=True) for side in range(2)], axis=0
+    )
     if tie:
         @pl.when(tie_recv)
         def _():
@@ -283,10 +294,7 @@
         for c in (1 - my_c,) if l is my_l else (my_c, 1 - my_c):
             col_copy(l, c).start()
 
-    best = jnp.concatenate(
-        [jnp.max(row_acc[0, side].T, axis=0, keepdims=True) for side in range(2)], axis=0
-    )
-    best = jnp.maximum(best, col_out[my_l, my_c])
+    best = jnp.maximum(own_best, col_out[my_l, my_c])
     for l, c in remote:
         await_col(l, c)
         best = jnp.maximum(best, col_in[l, c])
@@ -332,11 +340,13 @@
         functools.partial(kernel, n_row, n_col),
         out_shape=jax.ShapeDtypeStruct((2, rows), jnp.float32),
         in_specs=[
-            pl.BlockSpec(memory_space=pltpu.VMEM),
+            pl.BlockSpec(memory_space=pl.ANY),
             pl.BlockSpec(memory_space=pltpu.SMEM),
         ],
         out_specs=pl.BlockSpec(memory_space=pltpu.VMEM),
         scratch_shapes=[
+            pltpu.VMEM((rows, seg_len), jnp.float32),
+            dma((CHUNKS,)),
             pltpu.VMEM((n_row, 2 * rows, seg_len), jnp.bfloat16),
             pltpu.VMEM((slots, rows, seg_len), jnp.bfloat16),
             pltpu.VMEM((slots + 1, 2, rows, 128), jnp.float32),
@@ -355,7 +365,7 @@
             dma((slots,)),
         ],
         compiler_params=pltpu.CompilerParams(
-            collective_id=0, has_side_effects=True, vmem_limit_bytes=48 * 1024 * 1024
+            collective_id=0, has_side_effects=True, vmem_limit_bytes=60 * 1024 * 1024
         ),
         cost_estimate=pl.CostEstimate(
             flops=2 * rows * 2 * rows * n_row * seg_len * (slots + 1),

time: 37.2 us -> 34.8 us (0.935)
  Pallas kernels: 34.6 us -> 32.7 us
  local copies, waits for them, and re-layouts: 1.71 us -> 1.26 us
    pallas_call x1, Pallas kernels: 34.6 us -> 32.7 us  [shards(): pl.pallas_call(functools.partial(kernel, n_row, n_col), out_shape=jax.Sha...]
    unnamed x3 -> x1, local copies, waits for them, and re-layouts: 1.71 us -> 1.26 us
where the time goes in v2:
time: 34.8 us; the launch traced here: 34.6 us
  Pallas kernels  32.7 us (94%)
  local copies, waits for them, and re-layouts  1.26 us (4%)
  between operations  0.66 us (2%)
    pallas_call x1, Pallas kernels, shards(): pl.pallas_call(functools.partial(kernel, n_row, n_col), out_shape=jax.Sha...  32.7 us
    unnamed x1, local copies, waits for them, and re-layouts  1.26 us

profile of v2, /device:TPU:0, one launch (start us, length us, event | category | flops | bytes accessed | tf_op | source)
XLA Modules:
  0.0 34.6 jit_solution(10633453927206109492)
XLA Ops:
  0.7 32.7 %shard_map.28 = f32[2,384]{1,0:T(2,128)} custom-call(f32[384,512]{1,0:T(8,128)} %seg_hbm.1, s32[1]{0:T(128)S(6)} %copy.4.exclusion_ref), custom_call_target="tpu_custom_call" | custom-call | flops 3623878656 | bytes 786432 | tf_op jit(solution)/shard_map/pallas_call | solution.py:339
  33.4 1.3 %copy.5 = f32[2,384]{1,0:T(2,128)} copy(f32[2,384]{1,0:T(2,128)} %shard_map.28) | data formatting | bytes 6144

commit v3 on v2

--- a/solution.py
+++ b/solution.py
@@ -17,7 +17,7 @@
 def kernel(
     n_row, n_col, seg_hbm, exclusion_ref, out_ref, seg_ref, in_sem, plane, line, row_acc, col_acc,
     col_out, col_in, row_out, row_in, plane_recv, line_recv, col_recv, row_recv,
-    data_send, line_send, col_send, row_send,
+    data_send, line_send, col_send, row_send, pass_send,
 ):
     rows, seg_len = seg_ref.shape
     n_z = n_col // 2
@@ -42,6 +42,8 @@
     tie_recv = (my_z % max(tie, 1) + upper) % 2 == 1
     tie_send = (my_z % max(tie, 1) + upper) % 2 == 0
     forwarding = n_row == 4
+    passing = n_z == 4
+    passes = my_z == 1
     if forwarding:
         x_peer = my_l + 1 - 2 * (my_l % 2)
         y_peer = my_l + 2 - 4 * (my_l // 2)
@@ -98,8 +100,24 @@
         return pltpu.make_async_remote_copy(
             src_ref=part(my_l, my_c, k), dst_ref=line.at[i, pl.ds(k * step, step), :],
             send_sem=line_send.at[i, k], recv_sem=line_recv.at[i, k],
-            device_id=device(my_l, (my_z + n_z - d) % n_z, my_c), device_id_type=MESH,
-        )
+            device_id=device(my_l, (my_z + d) % n_z, my_c), device_id_type=MESH,
+        )
+
+    def pass_copy(i, k):
+        src = line.at[i, pl.ds(k * step, step), :]
+        return pltpu.make_async_remote_copy(
+            src_ref=src, dst_ref=line.at[1 - i, pl.ds(k * step, step), :],
+            send_sem=pass_send.at[i, k], recv_sem=line_recv.at[1 - i, k],
+            device_id=device(my_l, 2 - 2 * i, my_c), device_id_type=MESH,
+        )
+
+    def pass_on(k):
+        if passing:
+            @pl.when(passes)
+            def _():
+                for i in range(2):
+                    await_line(i, k)
+                    pass_copy(i, k).start()
 
     normalise(0)
     pl.semaphore_wait(barrier, len(greeted))
@@ -107,13 +125,22 @@
     for k in range(CHUNKS):
         if k:
             normalise(k)
-        for i, d in enumerate(shifts):
-            if d != tie:
-                line_copy(i, k).start()
+        if passing:
+            @pl.when(my_z != 3)
+            def _():
+                line_copy(0, k).start()
+
+            @pl.when(my_z == 3)
+            def _():
+                line_copy(1, k).start()
+        else:
+            for i, d in enumerate(shifts):
+                if d != tie:
+                    line_copy(i, k).start()
         for l in peers[:2] if forwarding else peers:
             send_part(my_l, my_c, k, device(l, my_z, my_c))
         send_part(my_l, my_c, k, sibling)
-    if tie:
+    if tie and not passing:
         @pl.when(tie_send)
         def _():
             for k in range(CHUNKS):
@@ -182,10 +209,10 @@
         d = shifts[i]
         near = False
         if min(d, n_z - d) == 1:
-            gap = (l - my_l) * n_z + my_z - (my_z + d) % n_z
+            gap = (l - my_l) * n_z + my_z - (my_z + n_z - d) % n_z
             near = (gap >= -1) & (gap <= 1)
         block(
-            lambda span: line[i, span, :], i + 1, (my_z + d) % n_z,
+            lambda span: line[i, span, :], i + 1, (my_z + n_z - d) % n_z,
             first, count, l, width, near, True,
         )
 
@@ -206,6 +233,7 @@
             if k >= CHUNKS // 2:
                 send_part(y_peer, my_c, k, device(x_peer, my_z, my_c))
             send_part(y_peer, my_c, k, sibling)
+            pass_on(k)
         early, late = peers[:2], peers[2:]
     else:
         early, late = peers, []
@@ -213,6 +241,8 @@
             for k in range(CHUNKS):
                 await_part(l, my_c, k)
                 send_part(l, my_c, k, sibling)
+        for k in range(CHUNKS):
+            pass_on(k)
     for l in early:
         for k in range(CHUNKS):
             await_part(l, 1 - my_c, k)
@@ -225,7 +255,10 @@
     whole = [i for i, d in enumerate(shifts) if d != tie]
     for i in whole:
         for k in range(CHUNKS):
-            await_line(i, k)
+            if passing:
+                pl.when(jnp.logical_not(passes))(functools.partial(await_line, i, k))
+            else:
+                await_line(i, k)
         for l in [my_l] + early:
             line_with(i, l, 0, rows, TILE)
     for l in late:
@@ -249,7 +282,7 @@
         return pltpu.make_async_remote_copy(
             src_ref=row_out.at[i], dst_ref=row_in.at[i], send_sem=row_send.at[i],
             recv_sem=row_recv.at[i],
-            device_id=device(my_l, (my_z + shifts[i]) % n_z, my_c), device_id_type=MESH,
+            device_id=device(my_l, (my_z + n_z - shifts[i]) % n_z, my_c), device_id_type=MESH,
         )
 
     for i in whole:
@@ -262,7 +295,10 @@
         def _():
             i = len(shifts) - 1
             for k in range(CHUNKS):
-                await_line(i, k)
+                if passing:
+                    pl.when(jnp.logical_not(passes))(functools.partial(await_line, i, k))
+                else:
+                    await_line(i, k)
 
                 def each(o, carry):
                     line_with(i, o, k * step, step, 2 * rows)
@@ -312,16 +348,35 @@
     for copy in started:
         copy.wait_send()
     for i in whole:
-        for k in range(CHUNKS):
-            line_copy(i, k).wait_send()
         row_copy(i).wait_send()
+    if passing:
+        @pl.when(passes)
+        def _():
+            for i in range(2):
+                for k in range(CHUNKS):
+                    pass_copy(i, k).wait_send()
+
+        @pl.when(my_z != 3)
+        def _():
+            for k in range(CHUNKS):
+                line_copy(0, k).wait_send()
+
+        @pl.when(my_z == 3)
+        def _():
+            for k in range(CHUNKS):
+                line_copy(1, k).wait_send()
+    else:
+        for i in whole:
+            for k in range(CHUNKS):
+                line_copy(i, k).wait_send()
     for l, c in remote:
         col_copy(l, c).wait_send()
     if tie:
-        @pl.when(tie_send)
-        def _():
-            for k in range(CHUNKS):
-                line_copy(len(shifts) - 1, k).wait_send()
+        if not passing:
+            @pl.when(tie_send)
+            def _():
+                for k in range(CHUNKS):
+                    line_copy(len(shifts) - 1, k).wait_send()
 
         @pl.when(tie_recv)
         def _():
@@ -340,7 +395,7 @@
         functools.partial(kernel, n_row, n_col),
         out_shape=jax.ShapeDtypeStruct((2, rows), jnp.float32),
         in_specs=[
-            pl.BlockSpec(memory_space=pl.ANY),
+            pl.BlockSpec(memory_space=pltpu.HBM),
             pl.BlockSpec(memory_space=pltpu.SMEM),
         ],
         out_specs=pl.BlockSpec(memory_space=pltpu.VMEM),
@@ -363,9 +418,10 @@
             dma((slots, CHUNKS)),
             dma((n_row, 2)),
             dma((slots,)),
+            dma((2, CHUNKS)),
         ],
         compiler_params=pltpu.CompilerParams(
-            collective_id=0, has_side_effects=True, vmem_limit_bytes=60 * 1024 * 1024
+            collective_id=0, has_side_effects=True, vmem_limit_bytes=48 * 1024 * 1024
         ),
         cost_estimate=pl.CostEstimate(
             flops=2 * rows * 2 * rows * n_row * seg_len * (slots + 1),

time: 34.8 us -> 35.7 us (1.026)
  local copies, waits for them, and re-layouts: 1.26 us -> 1.71 us
  Pallas kernels: 32.7 us -> 33.1 us
    unnamed x1 -> x3, local copies, waits for them, and re-layouts: 1.26 us -> 1.71 us
    pallas_call x1, Pallas kernels: 32.7 us -> 33.1 us  [shards(): pl.pallas_call(functools.partial(kernel, n_row, n_col), out_shape=jax.Sha...]
where the time goes in v3:
time: 35.7 us; the launch traced here: 35.5 us
  Pallas kernels  33.1 us (93%)
  local copies, waits for them, and re-layouts  1.71 us (5%)
  between operations  0.67 us (2%)
    pallas_call x1, Pallas kernels, shards(): pl.pallas_call(functools.partial(kernel, n_row, n_col), out_shape=jax.Sha...  33.1 us
    unnamed x3, local copies, waits for them, and re-layouts  1.71 us

profile of v3, /device:TPU:0, one launch (start us, length us, event | category | flops | bytes accessed | tf_op | source)
XLA Modules:
  0.0 35.5 jit_solution(14988136496547515418)
XLA Ops:
  0.7 0.0 copy-start
  0.7 1.1 %copy-done = f32[384,512]{1,0:T(8,128)S(1)} copy-done((f32[384,512]{1,0:T(8,128)S(1)}, f32[384,512]{1,0:T(8,128)}, u32[]{:S(2)}) %copy-start) | copy-done | bytes 786456
  1.8 33.1 %shard_map.28 = f32[2,384]{1,0:T(2,128)S(1)} custom-call(f32[384,512]{1,0:T(8,128)S(1)} %copy-done, s32[1]{0:T(128)S(6)} %copy.4.exclusion_ref), custom_call_target="tpu_custom_call" | custom-call | flops 3623878656 | bytes 786432 | tf_op jit(solution)/shard_map/pallas_call | solution.py:394
  34.9 0.6 %copy.5 = f32[2,384]{1,0:T(2,128)} copy(f32[2,384]{1,0:T(2,128)S(1)} %shard_map.28) | data formatting | bytes 6144
Async XLA Ops:
  0.7 1.1 %copy-start = (f32[384,512]{1,0:T(8,128)S(1)}, f32[384,512]{1,0:T(8,128)}, u32[]{:S(2)}) copy-start(f32[384,512]{1,0:T(8,128)} %seg_hbm.1) | copy-start | bytes 2359300

commit v4 on v2

v4 whole, which is shorter than its diff:
```python
import functools
import math

import jax
import jax.numpy as jnp
from jax import lax
from jax.experimental import pallas as pl
from jax.experimental.pallas import tpu as pltpu
from jax.sharding import PartitionSpec as P

MESH = pl.DeviceIdType.MESH
NONE = -3.0
CHUNKS = 4
TILE = 256


def kernel(
    n_row, n_col, seg_hbm, exclusion_ref, out_ref, seg_ref, in_sem, plane, line, line_acc,
    plane_acc, tie_rows, tie_cols, line_out, line_in, plane_out, plane_in, plane_recv, line_recv,
    msg_plane_recv, msg_line_recv, data_send, line_send, pair_send, pass_send, msg_plane_send,
    msg_line_send,
):
    rows, seg_len = seg_ref.shape
    n_z = n_col // 2
    step = rows // CHUNKS
    my_l = lax.axis_index("row")
    my_col = lax.axis_index("col")
    my_z = my_col // 2
    my_c = my_col % 2
    loads = [
        pltpu.make_async_copy(
            seg_hbm.at[pl.ds(k * step, step), :], seg_ref.at[pl.ds(k * step, step), :], in_sem.at[k]
        )
        for k in range(CHUNKS)
    ]
    for load in loads:
        load.start()
    shifts = list(range(1, (n_z - 1) // 2 + 1))
    tie = n_z // 2 if n_z % 2 == 0 else 0
    upper = my_z // max(tie, 1)
    tie_recv = (my_z % max(tie, 1) + upper) % 2 == 1
    tie_send = (my_z % max(tie, 1) + upper) % 2 == 0
    forwarding = n_row == 4
    passing = n_z == 4
    passes = my_z == 1
    if forwarding:
        x_peer = my_l + 1 - 2 * (my_l % 2)
        y_peer = my_l + 2 - 4 * (my_l // 2)
        peers = [x_peer, y_peer, 3 - my_l]
    else:
        peers = [(my_l + o) % n_row for o in range(1, n_row)]

    def device(l, z, c):
        return (l, z * 2 + c)

    barrier = pltpu.get_barrier_semaphore()
    sibling = device(my_l, my_z, 1 - my_c)
    greeted = [sibling] + [device(l, my_z, my_c) for l in peers]
    for d in range(1, n_z):
        greeted.append(device(my_l, (my_z + d) % n_z, my_c))
        greeted.append(device(my_l, (my_z + d) % n_z, 1 - my_c))
    for target in greeted:
        pl.semaphore_signal(barrier, inc=1, device_id=target, device_id_type=MESH)

    def half(c, k):
        return pl.ds(pl.multiple_of(c * rows + k * step, 16), step)

    def normalise(k):
        loads[k].wait()
        span = pl.ds(k * step, step)
        samples = seg_ref[span, :]
        average = jnp.mean(samples, axis=1, keepdims=True)
        centered = samples - average
        spread_inv = lax.rsqrt(jnp.mean(centered * centered, axis=1, keepdims=True) + 1e-05) * (
            1.0 / math.sqrt(seg_len)
        )
        normed = (centered * spread_inv).astype(jnp.bfloat16)
        plane[my_l, span, :] = normed
        line[0, half(my_c, k), :] = normed

    started = []

    def plane_copy(l, k, send_sem, target):
        part = plane.at[l, pl.ds(k * step, step), :]
        return pltpu.make_async_remote_copy(
            src_ref=part, dst_ref=part, send_sem=send_sem,
            recv_sem=plane_recv.at[l, k], device_id=target, device_id_type=MESH,
        )

    def send_part(l, k, target):
        copy = plane_copy(l, k, data_send.at[len(started)], device(target, my_z, my_c))
        copy.start()
        started.append(copy)

    def await_part(l, k):
        plane_copy(l, k, data_send.at[0], sibling).wait_recv()

    def line_copy(s, k):
        return pltpu.make_async_remote_copy(
            src_ref=plane.at[my_l, pl.ds(k * step, step), :], dst_ref=line.at[s, half(my_c, k), :],
            send_sem=line_send.at[s, k], recv_sem=line_recv.at[s, my_c, k],
            device_id=device(my_l, (my_z + s) % n_z, my_c), device_id_type=MESH,
        )

    def pair_copy(s, k):
        part = line.at[s, half(my_c, k), :]
        return pltpu.make_async_remote_copy(
            src_ref=part, dst_ref=part, send_sem=pair_send.at[s, k],
            recv_sem=line_recv.at[s, my_c, k], device_id=sibling, device_id_type=MESH,
        )

    def await_line(s, c, k):
        part = line.at[s, half(c, k), :]
        pltpu.make_async_remote_copy(
            src_ref=part, dst_ref=part, send_sem=pair_send.at[s, k],
            recv_sem=line_recv.at[s, c, k], device_id=sibling, device_id_type=MESH,
        ).wait_recv()

    def pass_copy(s, k):
        return pltpu.make_async_remote_copy(
            src_ref=line.at[s, half(my_c, k), :], dst_ref=line.at[3 - s, half(my_c, k), :],
            send_sem=pass_send.at[s - 1, k], recv_sem=line_recv.at[3 - s, my_c, k],
            device_id=device(my_l, 4 - 2 * s, my_c), device_id_type=MESH,
        )

    def take_line(s, k):
        await_line(s, my_c, k)
        pair_copy(s, k).start()

    normalise(0)
    pl.semaphore_wait(barrier, len(greeted))
    for k in range(CHUNKS):
        if k:
            normalise(k)
        if passing:
            pl.when(my_z != 3)(lambda: line_copy(1, k).start())
            pl.when(my_z == 3)(lambda: line_copy(2, k).start())
        else:
            for s in shifts:
                line_copy(s, k).start()
        for l in peers[:2] if forwarding else peers:
            send_part(my_l, k, l)
        pair_copy(0, k).start()
    if tie and not passing:
        @pl.when(tie_send)
        def _():
            for k in range(CHUNKS):
                line_copy(tie, k).start()

    line_acc[...] = jnp.full(line_acc.shape, NONE, jnp.float32)
    plane_acc[...] = jnp.full(plane_acc.shape, NONE, jnp.float32)
    tie_rows[...] = jnp.full(tie_rows.shape, NONE, jnp.float32)
    tie_cols[...] = jnp.full(tie_cols.shape, NONE, jnp.float32)
    exclude = exclusion_ref[0]

    def dot(a, b):
        return lax.dot_general(
            a, b, (((1,), (1,)), ((), ())), preferred_element_type=jnp.float32
        )

    def lanes(values):
        best = values[:, :128]
        for g in range(1, values.shape[1] // 128):
            best = jnp.maximum(best, values[:, g * 128 : (g + 1) * 128])
        return best

    def sublanes(values):
        return jnp.max(values.reshape(values.shape[0] // 8, 8, values.shape[1]), axis=0)

    def gap_of(s, l):
        return (l - my_l) * n_z + my_z - (my_z + n_z - s) % n_z

    def block(s, l):
        gap = gap_of(s, l)

        def keep(side, cols, values):
            line_acc[s, side, :, cols] = jnp.maximum(line_acc[s, side, :, cols], sublanes(values))
            if s:
                plane_acc[l, 1 - side] = jnp.maximum(plane_acc[l, 1 - side], lanes(values))

        def masked():
            for begin in range(0, 2 * rows, TILE):
                cols = pl.ds(begin, TILE)
                p = dot(plane[l], line[s, cols, :])
                apart = (gap * 2 * rows + my_c * rows - begin) + (
                    lax.broadcasted_iota(jnp.int32, p.shape, 0)
                    - lax.broadcasted_iota(jnp.int32, p.shape, 1)
                )
                keep(1, cols, jnp.where(apart > exclude, p, NONE))
                keep(0, cols, jnp.where(apart < -exclude, p, NONE))

        def plain():
            side = (gap > 0).astype(jnp.int32)
            for begin in range(0, 2 * rows, TILE):
                cols = pl.ds(begin, TILE)
                keep(side, cols, dot(plane[l], line[s, cols, :]))

        if s == 0:
            masked() if n_z == 1 or l is my_l else plain()
        elif min(s, n_z - s) == 1:
            near = (gap >= -1) & (gap <= 1)
            pl.when(near)(masked)
            pl.when(jnp.logical_not(near))(plain)
        else:
            plain()

    for k in range(CHUNKS):
        await_line(0, 1 - my_c, k)
    block(0, my_l)
    if forwarding:
        for k in range(CHUNKS):
            await_part(x_peer, k)
            if k < CHUNKS // 2:
                send_part(x_peer, k, y_peer)
            await_part(y_peer, k)
            if k >= CHUNKS // 2:
                send_part(y_peer, k, x_peer)
            if passing:
                @pl.when(my_z != 0)
                def _():
                    take_line(1, k)

                @pl.when(passes)
                def _():
                    pass_copy(1, k).start()
                    take_line(2, k)
                    pass_copy(2, k).start()
        early, late = peers[:2], peers[2:]
    else:
        early, late = peers, []
        for l in early:
            for k in range(CHUNKS):
                await_part(l, k)
        if passing:
            for k in range(CHUNKS):
                @pl.when(my_z != 0)
                def _():
                    take_line(1, k)

                @pl.when(passes)
                def _():
                    pass_copy(1, k).start()
                    take_line(2, k)
                    pass_copy(2, k).start()
    for l in early:
        block(0, l)
    for s in shifts:
        for k in range(CHUNKS):
            if passing:
                pl.when(my_z == 0)(functools.partial(take_line, s, k))
            else:
                take_line(s, k)
        for k in range(CHUNKS):
            await_line(s, 1 - my_c, k)
        for l in [my_l] + early:
            block(s, l)
    for l in late:
        for k in range(CHUNKS):
            await_part(l, k)
        for s in [0] + shifts:
            block(s, l)

    def msg_line_copy(s, c):
        return pltpu.make_async_remote_copy(
            src_ref=line_out.at[s, c], dst_ref=line_in.at[s, my_c],
            send_sem=msg_line_send.at[s, c], recv_sem=msg_line_recv.at[s, my_c],
            device_id=device(my_l, (my_z + n_z - s) % n_z, c), device_id_type=MESH,
        )

    def await_msg_line(s, c):
        pltpu.make_async_remote_copy(
            src_ref=line_out.at[s, c], dst_ref=line_in.at[s, c],
            send_sem=msg_line_send.at[s, c], recv_sem=msg_line_recv.at[s, c],
            device_id=sibling, device_id_type=MESH,
        ).wait_recv()

    for s in [0] + shifts:
        for side in range(2):
            best = jnp.max(line_acc[s, side], axis=0, keepdims=True)
            for c in range(2):
                line_out[s, c, side : side + 1, :] = best[:, c * rows : (c + 1) * rows]
        for c in (my_c, 1 - my_c) if s else (1 - my_c,):
            msg_line_copy(s, c).start()
    if shifts:
        for l in range(n_row):
            for side in range(2):
                plane_out[l, side : side + 1, :] = jnp.max(
                    plane_acc[l, side].T, axis=0, keepdims=True
                )
    else:
        plane_out[...] = jnp.full(plane_out.shape, NONE, jnp.float32)

    if tie:
        @pl.when(tie_recv)
        def _():
            done = 0
            for k in range(CHUNKS):
                if passing:
                    pl.when(jnp.logical_not(passes))(functools.partial(take_line, tie, k))
                else:
                    take_line(tie, k)
                await_line(tie, 1 - my_c, k)
                spans = [pl.ds(c * rows + k * step, step) for c in range(2)]
                data = jnp.concatenate([line[tie, span, :] for span in spans], axis=0)
                for l in range(n_row):
                    p = dot(data, plane[l])
                    gap = gap_of(tie, l)

                    def keep(side, line_values, plane_values):
                        best = lanes(line_values)
                        for c, span in enumerate(spans):
                            tie_rows[side, span, :] = jnp.maximum(
                                tie_rows[side, span, :], best[c * step : (c + 1) * step]
                            )
                        tie_cols[l, 1 - side] = jnp.maximum(
                            tie_cols[l, 1 - side], sublanes(plane_values)
                        )

                    if min(tie, n_z - tie) == 1:
                        index = lax.broadcasted_iota(jnp.int32, p.shape, 0)
                        index = jnp.where(index >= step, index + (rows - step), index) + k * step
                        apart = (gap * 2 * rows + my_c * rows) + (
                            lax.broadcasted_iota(jnp.int32, p.shape, 1) - index
                        )
                        later = jnp.where(apart > exclude, p, NONE)
                        earlier = jnp.where(apart < -exclude, p, NONE)
                        keep(1, later, later)
                        keep(0, earlier, earlier)
                    else:
                        keep((gap > 0).astype(jnp.int32), p, p)
                upto = (k + 1) * step // 128 * 128
                if upto > done:
                    for c in range(2):
                        for side in range(2):
                            line_out[tie, c, side : side + 1, done:upto] = jnp.max(
                                tie_rows[side, c * rows + done : c * rows + upto, :].T,
                                axis=0, keepdims=True,
                            )
                    done = upto
            for c in (my_c, 1 - my_c):
                msg_line_copy(tie, c).start()
            for l in range(n_row):
                for side in range(2):
                    plane_out[l, side : side + 1, :] = jnp.maximum(
                        plane_out[l, side : side + 1, :],
                        jnp.max(tie_cols[l, side], axis=0, keepdims=True),
                    )

    def msg_plane_copy(l):
        return pltpu.make_async_remote_copy(
            src_ref=plane_out.at[l], dst_ref=plane_in.at[my_l],
            send_sem=msg_plane_send.at[l], recv_sem=msg_plane_recv.at[my_l],
            device_id=device(l, my_z, my_c), device_id_type=MESH,
        )

    def await_msg_plane(l):
        pltpu.make_async_remote_copy(
            src_ref=plane_out.at[l], dst_ref=plane_in.at[l],
            send_sem=msg_plane_send.at[l], recv_sem=msg_plane_recv.at[l],
            device_id=sibling, device_id_type=MESH,
        ).wait_recv()

    for l in peers:
        msg_plane_copy(l).start()
    best = jnp.maximum(line_out[0, my_c], plane_out[my_l])
    await_msg_line(0, 1 - my_c)
    best = jnp.maximum(best, line_in[0, 1 - my_c])
    for s in shifts:
        for c in range(2):
            await_msg_line(s, c)
            best = jnp.maximum(best, line_in[s, c])
    for l in peers:
        await_msg_plane(l)
        best = jnp.maximum(best, plane_in[l])
    out_ref[...] = 1.0 - best
    if tie:
        @pl.when(tie_send)
        def _():
            for c in range(2):
                await_msg_line(tie, c)
            out_ref[...] = jnp.minimum(
                out_ref[...], 1.0 - jnp.maximum(line_in[tie, 0], line_in[tie, 1])
            )

    for copy in started:
        copy.wait_send()
    for k in range(CHUNKS):
        pair_copy(0, k).wait_send()
        for s in shifts:
            pair_copy(s, k).wait_send()
    msg_line_copy(0, 1 - my_c).wait_send()
    for s in shifts:
        for c in range(2):
            msg_line_copy(s, c).wait_send()
    for l in peers:
        msg_plane_copy(l).wait_send()
    if passing:
        @pl.when(passes)
        def _():
            for s in (1, 2):
                for k in range(CHUNKS):
                    pass_copy(s, k).wait_send()

        @pl.when(my_z != 3)
        def _():
            for k in range(CHUNKS):
                line_copy(1, k).wait_send()

        @pl.when(my_z == 3)
        def _():
            for k in range(CHUNKS):
                line_copy(2, k).wait_send()
    else:
        for s in shifts:
            for k in range(CHUNKS):
                line_copy(s, k).wait_send()
    if tie:
        if not passing:
            @pl.when(tie_send)
            def _():
                for k in range(CHUNKS):
                    line_copy(tie, k).wait_send()

        @pl.when(tie_recv)
        def _():
            for k in range(CHUNKS):
                pair_copy(tie, k).wait_send()
            for c in range(2):
                msg_line_copy(tie, c).wait_send()


def shards(segments, exclusion):
    rows, seg_len = segments.shape
    n_row = lax.axis_size("row")
    n_col = lax.axis_size("col")
    slots = n_col // 4 + 1
    dma = pltpu.SemaphoreType.DMA
    return pl.pallas_call(
        functools.partial(kernel, n_row, n_col),
        out_shape=jax.ShapeDtypeStruct((2, rows), jnp.float32),
        in_specs=[
            pl.BlockSpec(memory_space=pl.ANY),
            pl.BlockSpec(memory_space=pltpu.SMEM),
        ],
        out_specs=pl.BlockSpec(memory_space=pltpu.VMEM),
        scratch_shapes=[
            pltpu.VMEM((rows, seg_len), jnp.float32),
            dma((CHUNKS,)),
            pltpu.VMEM((n_row, rows, seg_len), jnp.bfloat16),
            pltpu.VMEM((slots, 2 * rows, seg_len), jnp.bfloat16),
            pltpu.VMEM((slots, 2, 8, 2 * rows), jnp.float32),
            pltpu.VMEM((n_row, 2, rows, 128), jnp.float32),
            pltpu.VMEM((2, 2 * rows, 128), jnp.float32),
            pltpu.VMEM((n_row, 2, 8, rows), jnp.float32),
            pltpu.VMEM((slots, 2, 2, rows), jnp.float32),
            pltpu.VMEM((slots, 2, 2, rows), jnp.float32),
            pltpu.VMEM((n_row, 2, rows), jnp.float32),
            pltpu.VMEM((n_row, 2, rows), jnp.float32),
            dma((n_row, CHUNKS)),
            dma((slots, 2, CHUNKS)),
            dma((n_row,)),
            dma((slots, 2)),
            dma((CHUNKS * n_row,)),
            dma((slots, CHUNKS)),
            dma((slots, CHUNKS)),
            dma((2, CHUNKS)),
            dma((n_row,)),
            dma((slots, 2)),
        ],
        compiler_params=pltpu.CompilerParams(
            collective_id=0, has_side_effects=True, vmem_limit_bytes=55900000
        ),
        cost_estimate=pl.CostEstimate(
            flops=2 * rows * 2 * rows * n_row * seg_len * slots,
            bytes_accessed=rows * seg_len * 4,
            transcendentals=0,
        ),
    )(segments, exclusion)


def solution(mesh):
    return jax.shard_map(
        shards,
        mesh=mesh,
        in_specs=(P(("row", "col"), None), P()),
        out_specs=P(None, ("row", "col")),
        check_vma=False,
    )
```

time: 34.8 us -> 34 us (0.977)
  local copies, waits for them, and re-layouts: 1.26 us -> 0.58 us
    unnamed x1, local copies, waits for them, and re-layouts: 1.26 us -> 0.58 us
where the time goes in v4:
time: 34 us; the launch traced here: 33.8 us
  Pallas kernels  32.6 us (96%)
  between operations  0.66 us (2%)
  local copies, waits for them, and re-layouts  0.58 us (2%)
    pallas_call x1, Pallas kernels, shards(): pl.pallas_call(functools.partial(kernel, n_row, n_col), out_shape=jax.Sha...  32.6 us

profile of v4, /device:TPU:0, one launch (start us, length us, event | category | flops | bytes accessed | tf_op | source)
XLA Modules:
  0.0 33.8 jit_solution(10785613723993423134)
XLA Ops:
  0.7 32.6 %shard_map.28 = f32[2,384]{1,0:T(2,128)S(1)} custom-call(f32[384,512]{1,0:T(8,128)} %seg_hbm.1, s32[1]{0:T(128)S(6)} %copy.4.exclusion_ref), custom_call_target="tpu_custom_call" | custom-call | flops 3623878656 | bytes 786432 | tf_op jit(solution)/shard_map/pallas_call | solution.py:438
  33.2 0.6 %copy.5 = f32[2,384]{1,0:T(2,128)} copy(f32[2,384]{1,0:T(2,128)S(1)} %shard_map.28) | data formatting | bytes 6144

commit v5 on v4

--- a/solution.py
+++ b/solution.py
@@ -138,8 +138,10 @@
         else:
             for s in shifts:
                 line_copy(s, k).start()
+    for k in range(CHUNKS):
         for l in peers[:2] if forwarding else peers:
             send_part(my_l, k, l)
+    for k in range(CHUNKS):
         pair_copy(0, k).start()
     if tie and not passing:
         @pl.when(tie_send)
@@ -207,47 +209,42 @@
     for k in range(CHUNKS):
         await_line(0, 1 - my_c, k)
     block(0, my_l)
+    early, late = (peers[:2], peers[2:]) if forwarding else (peers, [])
+    for k in range(CHUNKS):
+        if passing:
+            @pl.when(passes)
+            def _():
+                await_line(1, my_c, k)
+                pass_copy(1, k).start()
+                pair_copy(1, k).start()
+
+        if forwarding and k < CHUNKS // 2:
+            await_part(x_peer, k)
+            send_part(x_peer, k, y_peer)
     if forwarding:
-        for k in range(CHUNKS):
-            await_part(x_peer, k)
-            if k < CHUNKS // 2:
-                send_part(x_peer, k, y_peer)
+        for k in range(CHUNKS // 2, CHUNKS):
             await_part(y_peer, k)
-            if k >= CHUNKS // 2:
-                send_part(y_peer, k, x_peer)
-            if passing:
-                @pl.when(my_z != 0)
-                def _():
-                    take_line(1, k)
-
-                @pl.when(passes)
-                def _():
-                    pass_copy(1, k).start()
-                    take_line(2, k)
-                    pass_copy(2, k).start()
-        early, late = peers[:2], peers[2:]
-    else:
-        early, late = peers, []
-        for l in early:
-            for k in range(CHUNKS):
+            send_part(y_peer, k, x_peer)
+    for k in range(CHUNKS):
+        if passing:
+            @pl.when(passes)
+            def _():
+                take_line(2, k)
+                pass_copy(2, k).start()
+
+        if not forwarding:
+            for l in early:
                 await_part(l, k)
-        if passing:
-            for k in range(CHUNKS):
-                @pl.when(my_z != 0)
-                def _():
-                    take_line(1, k)
-
-                @pl.when(passes)
-                def _():
-                    pass_copy(1, k).start()
-                    take_line(2, k)
-                    pass_copy(2, k).start()
+    if forwarding:
+        for k in range(CHUNKS // 2):
+            await_part(x_peer, k + CHUNKS // 2)
+            await_part(y_peer, k)
     for l in early:
         block(0, l)
     for s in shifts:
         for k in range(CHUNKS):
             if passing:
-                pl.when(my_z == 0)(functools.partial(take_line, s, k))
+                pl.when(jnp.logical_not(passes))(functools.partial(take_line, s, k))
             else:
                 take_line(s, k)
         for k in range(CHUNKS):

time: 34 us -> 35.1 us (1.032)
  Pallas kernels: 32.6 us -> 33.8 us
    pallas_call x1, Pallas kernels: 32.6 us -> 33.8 us  [shards(): pl.pallas_call(functools.partial(kernel, n_row, n_col), out_shape=jax.Sha...]
where the time goes in v5:
time: 35.1 us; the launch traced here: 35 us
  Pallas kernels  33.8 us (96%)
  between operations  0.66 us (2%)
  local copies, waits for them, and re-layouts  0.58 us (2%)
    pallas_call x1, Pallas kernels, shards(): pl.pallas_call(functools.partial(kernel, n_row, n_col), out_shape=jax.Sha...  33.8 us

profile of v5, /device:TPU:0, one launch (start us, length us, event | category | flops | bytes accessed | tf_op | source)
XLA Modules:
  0.0 35.0 jit_solution(16230441270106640389)
XLA Ops:
  0.7 33.8 %shard_map.28 = f32[2,384]{1,0:T(2,128)S(1)} custom-call(f32[384,512]{1,0:T(8,128)} %seg_hbm.1, s32[1]{0:T(128)S(6)} %copy.4.exclusion_ref), custom_call_target="tpu_custom_call" | custom-call | flops 3623878656 | bytes 786432 | tf_op jit(solution)/shard_map/pallas_call | solution.py:435
  34.4 0.6 %copy.5 = f32[2,384]{1,0:T(2,128)} copy(f32[2,384]{1,0:T(2,128)S(1)} %shard_map.28) | data formatting | bytes 6144

commit v6 on v5

v6 whole, which is shorter than its diff:
```python
import functools
import math

import jax
import jax.numpy as jnp
from jax import lax
from jax.experimental import pallas as pl
from jax.experimental.pallas import tpu as pltpu
from jax.sharding import PartitionSpec as P

MESH = pl.DeviceIdType.MESH
NONE = -3.0
CHUNKS = 4
PARTS = 3
TILE = 256


def kernel(
    n_row, n_col, seg_hbm, exclusion_ref, out_ref, seg_ref, in_sem, plane, line, line_acc,
    plane_acc, tie_acc, line_out, line_in, plane_out, plane_in, plane_recv, line_recv,
    msg_plane_recv, msg_line_recv, data_send, line_send, pair_send, pass_send, msg_plane_send,
    msg_line_send,
):
    rows, seg_len = seg_ref.shape
    n_z = n_col // 2
    step = rows // CHUNKS
    size = rows // PARTS
    my_l = lax.axis_index("row")
    my_col = lax.axis_index("col")
    my_z = my_col // 2
    my_c = my_col % 2
    loads = [
        pltpu.make_async_copy(
            seg_hbm.at[pl.ds(k * size, size), :], seg_ref.at[pl.ds(k * size, size), :], in_sem.at[k]
        )
        for k in range(PARTS)
    ]
    for load in loads:
        load.start()
    shifts = list(range(1, (n_z - 1) // 2 + 1))
    tie = n_z // 2 if n_z % 2 == 0 else 0
    upper = my_z // max(tie, 1)
    tie_recv = (my_z % max(tie, 1) + upper) % 2 == 1
    tie_send = (my_z % max(tie, 1) + upper) % 2 == 0
    forwarding = n_row == 4
    passing = n_z == 4
    passes = my_z == 1
    if forwarding:
        x_peer = my_l + 1 - 2 * (my_l % 2)
        y_peer = my_l + 2 - 4 * (my_l // 2)
        peers = [x_peer, y_peer, 3 - my_l]
    else:
        peers = [(my_l + o) % n_row for o in range(1, n_row)]

    def device(l, z, c):
        return (l, z * 2 + c)

    barrier = pltpu.get_barrier_semaphore()
    sibling = device(my_l, my_z, 1 - my_c)
    greeted = [sibling] + [device(l, my_z, my_c) for l in peers]
    for d in range(1, n_z):
        greeted.append(device(my_l, (my_z + d) % n_z, my_c))
        greeted.append(device(my_l, (my_z + d) % n_z, 1 - my_c))
    for target in greeted:
        pl.semaphore_signal(barrier, inc=1, device_id=target, device_id_type=MESH)

    def half(c, k):
        return pl.ds(pl.multiple_of(c * rows + k * size, 16), size)

    def normalise(k):
        loads[k].wait()
        span = pl.ds(k * size, size)
        samples = seg_ref[span, :]
        average = jnp.mean(samples, axis=1, keepdims=True)
        centered = samples - average
        spread_inv = lax.rsqrt(jnp.mean(centered * centered, axis=1, keepdims=True) + 1e-05) * (
            1.0 / math.sqrt(seg_len)
        )
        normed = (centered * spread_inv).astype(jnp.bfloat16)
        plane[span, :] = normed
        line[0, half(my_c, k), :] = normed

    started = []

    order = [my_l] + peers

    def back(j):
        return j if forwarding else (n_row - j) % n_row

    def plane_copy(src, dst, k, send_sem, target):
        return pltpu.make_async_remote_copy(
            src_ref=plane.at[pl.ds(src * rows + k * step, step), :],
            dst_ref=plane.at[pl.ds(dst * rows + k * step, step), :],
            send_sem=send_sem, recv_sem=plane_recv.at[dst, k],
            device_id=target, device_id_type=MESH,
        )

    def send_part(src, dst, k, j):
        copy = plane_copy(
            src, dst, k, data_send.at[len(started)], device(order[j], my_z, my_c)
        )
        copy.start()
        started.append(copy)

    def await_part(j, k):
        plane_copy(j, j, k, data_send.at[0], sibling).wait_recv()

    def line_copy(s, k):
        return pltpu.make_async_remote_copy(
            src_ref=plane.at[pl.ds(k * size, size), :], dst_ref=line.at[s, half(my_c, k), :],
            send_sem=line_send.at[s, k], recv_sem=line_recv.at[s, my_c, k],
            device_id=device(my_l, (my_z + s) % n_z, my_c), device_id_type=MESH,
        )

    def pair_copy(s, k):
        part = line.at[s, half(my_c, k), :]
        return pltpu.make_async_remote_copy(
            src_ref=part, dst_ref=part, send_sem=pair_send.at[s, k],
            recv_sem=line_recv.at[s, my_c, k], device_id=sibling, device_id_type=MESH,
        )

    def await_line(s, c, k):
        part = line.at[s, half(c, k), :]
        pltpu.make_async_remote_copy(
            src_ref=part, dst_ref=part, send_sem=pair_send.at[s, k],
            recv_sem=line_recv.at[s, c, k], device_id=sibling, device_id_type=MESH,
        ).wait_recv()

    def pass_copy(s, k):
        return pltpu.make_async_remote_copy(
            src_ref=line.at[s, half(my_c, k), :], dst_ref=line.at[3 - s, half(my_c, k), :],
            send_sem=pass_send.at[s - 1, k], recv_sem=line_recv.at[3 - s, my_c, k],
            device_id=device(my_l, 4 - 2 * s, my_c), device_id_type=MESH,
        )

    def take_line(s, k):
        await_line(s, my_c, k)
        pair_copy(s, k).start()

    normalise(0)
    pl.semaphore_wait(barrier, len(greeted))
    sent = 0
    for k in range(PARTS):
        if k:
            normalise(k)
        if passing:
            pl.when(my_z != 3)(lambda: line_copy(1, k).start())
            pl.when(my_z == 3)(lambda: line_copy(2, k).start())
        else:
            for s in shifts:
                line_copy(s, k).start()
        while (sent + 1) * step <= (k + 1) * size:
            for j in (1, 2) if forwarding else range(1, n_row):
                send_part(0, back(j), sent, j)
            sent += 1
        pair_copy(0, k).start()
    if tie and not passing:
        @pl.when(tie_send)
        def _():
            for k in range(PARTS):
                line_copy(tie, k).start()

    line_acc[...] = jnp.full(line_acc.shape, NONE, jnp.float32)
    plane_acc[...] = jnp.full(plane_acc.shape, NONE, jnp.float32)
    tie_acc[...] = jnp.full(tie_acc.shape, NONE, jnp.float32)
    exclude = exclusion_ref[0]

    def dot(a, b):
        return lax.dot_general(
            a, b, (((1,), (1,)), ((), ())), preferred_element_type=jnp.float32
        )

    def lanes(values):
        best = values[:, :128]
        for g in range(1, values.shape[1] // 128):
            best = jnp.maximum(best, values[:, g * 128 : (g + 1) * 128])
        return best

    def sublanes(values):
        return jnp.max(values.reshape(values.shape[0] // 8, 8, values.shape[1]), axis=0)

    def gap_of(s, l):
        return (l - my_l) * n_z + my_z - (my_z + n_z - s) % n_z

    def rows_of(j):
        return plane[j * rows : (j + 1) * rows, :]

    def block(s, j):
        gap = gap_of(s, order[j])

        def keep(side, cols, values):
            line_acc[s, side, :, cols] = jnp.maximum(line_acc[s, side, :, cols], sublanes(values))
            if s:
                plane_acc[j, 1 - side] = jnp.maximum(plane_acc[j, 1 - side], lanes(values))

        def masked():
            for begin in range(0, 2 * rows, TILE):
                cols = pl.ds(begin, TILE)
                p = dot(rows_of(j), line[s, cols, :])
                apart = (gap * 2 * rows + my_c * rows - begin) + (
                    lax.broadcasted_iota(jnp.int32, p.shape, 0)
                    - lax.broadcasted_iota(jnp.int32, p.shape, 1)
                )
                keep(1, cols, jnp.where(apart > exclude, p, NONE))
                keep(0, cols, jnp.where(apart < -exclude, p, NONE))

        def plain():
            side = (gap > 0).astype(jnp.int32)
            for begin in range(0, 2 * rows, TILE):
                cols = pl.ds(begin, TILE)
                keep(side, cols, dot(rows_of(j), line[s, cols, :]))

        if s == 0:
            masked() if n_z == 1 or j == 0 else plain()
        elif min(s, n_z - s) == 1:
            near = (gap >= -1) & (gap <= 1)
            pl.when(near)(masked)
            pl.when(jnp.logical_not(near))(plain)
        else:
            plain()

    def pass_on(k):
        if passing:
            @pl.when(my_z != 0)
            def _():
                take_line(1, k)

            @pl.when(passes)
            def _():
                pass_copy(1, k).start()
                take_line(2, k)
                pass_copy(2, k).start()

    for k in range(PARTS):
        await_line(0, 1 - my_c, k)
    block(0, 0)
    if forwarding:
        for k in range(CHUNKS):
            await_part(1, k)
            if k < CHUNKS // 2:
                send_part(1, 3, k, 2)
            await_part(2, k)
            if k >= CHUNKS // 2:
                send_part(2, 3, k, 1)
            if k < PARTS:
                pass_on(k)
        early, late = [1, 2], [3]
    else:
        early, late = list(range(1, n_row)), []
        for j in early:
            for k in range(CHUNKS):
                await_part(j, k)
        for k in range(PARTS):
            pass_on(k)
    for j in early:
        block(0, j)
    for s in shifts:
        for k in range(PARTS):
            if passing:
                pl.when(my_z == 0)(functools.partial(take_line, s, k))
            else:
                take_line(s, k)
        for k in range(PARTS):
            await_line(s, 1 - my_c, k)
        for j in [0] + early:
            block(s, j)
    for j in late:
        for k in range(CHUNKS):
            await_part(j, k)
        for s in [0] + shifts:
            block(s, j)

    def msg_line_copy(s, c):
        return pltpu.make_async_remote_copy(
            src_ref=line_out.at[s, c], dst_ref=line_in.at[s, my_c],
            send_sem=msg_line_send.at[s, c], recv_sem=msg_line_recv.at[s, my_c],
            device_id=device(my_l, (my_z + n_z - s) % n_z, c), device_id_type=MESH,
        )

    def await_msg_line(s, c):
        pltpu.make_async_remote_copy(
            src_ref=line_out.at[s, c], dst_ref=line_in.at[s, c],
            send_sem=msg_line_send.at[s, c], recv_sem=msg_line_recv.at[s, c],
            device_id=sibling, device_id_type=MESH,
        ).wait_recv()

    def send_line_maxima(s):
        for side in range(2):
            best = jnp.max(line_acc[s, side], axis=0, keepdims=True)
            for c in range(2):
                line_out[s, c, side : side + 1, :] = best[:, c * rows : (c + 1) * rows]
        for c in (my_c, 1 - my_c) if s else (1 - my_c,):
            msg_line_copy(s, c).start()

    for s in [0] + shifts:
        send_line_maxima(s)
    if shifts:
        for l in range(n_row):
            for side in range(2):
                plane_out[l, side : side + 1, :] = jnp.max(
                    plane_acc[l, side].T, axis=0, keepdims=True
                )
    else:
        plane_out[...] = jnp.full(plane_out.shape, NONE, jnp.float32)

    if tie:
        @pl.when(tie_recv)
        def _():
            adjacent = n_z == 2
            for k in range(PARTS):
                if passing:
                    pl.when(jnp.logical_not(passes))(functools.partial(take_line, tie, k))
                else:
                    take_line(tie, k)
                await_line(tie, 1 - my_c, k)
                spans = [pl.ds(c * rows + k * size, size) for c in range(2)]
                data = jnp.concatenate([line[tie, span, :] for span in spans], axis=0)
                products = dot(plane[...], data)
                for j in range(n_row):
                    p = products[j * rows : (j + 1) * rows]
                    gap = gap_of(tie, order[j])

                    def keep(side, slot, values):
                        best = sublanes(values)
                        for c, span in enumerate(spans):
                            line_acc[tie, side, :, span] = jnp.maximum(
                                line_acc[tie, side, :, span], best[:, c * size : (c + 1) * size]
                            )
                        tie_acc[j, slot] = jnp.maximum(tie_acc[j, slot], lanes(values))

                    if adjacent:
                        index = lax.broadcasted_iota(jnp.int32, p.shape, 1)
                        index = jnp.where(index >= size, index + (rows - size), index) + k * size
                        apart = (gap * 2 * rows + my_c * rows) + (
                            lax.broadcasted_iota(jnp.int32, p.shape, 0) - index
                        )
                        keep(1, 0, jnp.where(apart > exclude, p, NONE))
                        keep(0, 1, jnp.where(apart < -exclude, p, NONE))
                    else:
                        keep((gap > 0).astype(jnp.int32), 0, p)
            send_line_maxima(tie)
            for j in range(n_row):
                for slot in range(2 if adjacent else 1):
                    side = slot if adjacent else 1 - (gap_of(tie, order[j]) > 0).astype(jnp.int32)
                    best = jnp.max(tie_acc[j, slot].T, axis=0, keepdims=True)
                    plane_out[j, pl.ds(side, 1), :] = jnp.maximum(
                        plane_out[j, pl.ds(side, 1), :], best
                    )

    def msg_plane_copy(j):
        return pltpu.make_async_remote_copy(
            src_ref=plane_out.at[j], dst_ref=plane_in.at[back(j)],
            send_sem=msg_plane_send.at[j], recv_sem=msg_plane_recv.at[back(j)],
            device_id=device(order[j], my_z, my_c), device_id_type=MESH,
        )

    def await_msg_plane(j):
        pltpu.make_async_remote_copy(
            src_ref=plane_out.at[j], dst_ref=plane_in.at[j],
            send_sem=msg_plane_send.at[j], recv_sem=msg_plane_recv.at[j],
            device_id=sibling, device_id_type=MESH,
        ).wait_recv()

    for j in range(1, n_row):
        msg_plane_copy(j).start()
    best = jnp.maximum(line_out[0, my_c], plane_out[0])
    await_msg_line(0, 1 - my_c)
    best = jnp.maximum(best, line_in[0, 1 - my_c])
    for s in shifts:
        for c in range(2):
            await_msg_line(s, c)
            best = jnp.maximum(best, line_in[s, c])
    for j in range(1, n_row):
        await_msg_plane(j)
        best = jnp.maximum(best, plane_in[j])
    out_ref[...] = 1.0 - best
    if tie:
        @pl.when(tie_send)
        def _():
            for c in range(2):
                await_msg_line(tie, c)
            out_ref[...] = jnp.minimum(
                out_ref[...], 1.0 - jnp.maximum(line_in[tie, 0], line_in[tie, 1])
            )

    for copy in started:
        copy.wait_send()
    for k in range(PARTS):
        pair_copy(0, k).wait_send()
        for s in shifts:
            pair_copy(s, k).wait_send()
    msg_line_copy(0, 1 - my_c).wait_send()
    for s in shifts:
        for c in range(2):
            msg_line_copy(s, c).wait_send()
    for j in range(1, n_row):
        msg_plane_copy(j).wait_send()
    if passing:
        @pl.when(passes)
        def _():
            for s in (1, 2):
                for k in range(PARTS):
                    pass_copy(s, k).wait_send()

        @pl.when(my_z != 3)
        def _():
            for k in range(PARTS):
                line_copy(1, k).wait_send()

        @pl.when(my_z == 3)
        def _():
            for k in range(PARTS):
                line_copy(2, k).wait_send()
    else:
        for s in shifts:
            for k in range(PARTS):
                line_copy(s, k).wait_send()
    if tie:
        if not passing:
            @pl.when(tie_send)
            def _():
                for k in range(PARTS):
                    line_copy(tie, k).wait_send()

        @pl.when(tie_recv)
        def _():
            for k in range(PARTS):
                pair_copy(tie, k).wait_send()
            for c in range(2):
                msg_line_copy(tie, c).wait_send()


def shards(segments, exclusion):
    rows, seg_len = segments.shape
    n_row = lax.axis_size("row")
    n_col = lax.axis_size("col")
    slots = n_col // 4 + 1
    dma = pltpu.SemaphoreType.DMA
    return pl.pallas_call(
        functools.partial(kernel, n_row, n_col),
        out_shape=jax.ShapeDtypeStruct((2, rows), jnp.float32),
        in_specs=[
            pl.BlockSpec(memory_space=pl.ANY),
            pl.BlockSpec(memory_space=pltpu.SMEM),
        ],
        out_specs=pl.BlockSpec(memory_space=pltpu.VMEM),
        scratch_shapes=[
            pltpu.VMEM((rows, seg_len), jnp.float32),
            dma((PARTS,)),
            pltpu.VMEM((n_row * rows, seg_len), jnp.bfloat16),
            pltpu.VMEM((slots, 2 * rows, seg_len), jnp.bfloat16),
            pltpu.VMEM((slots, 2, 8, 2 * rows), jnp.float32),
            pltpu.VMEM((n_row, 2, rows, 128), jnp.float32),
            pltpu.VMEM((n_row, 2, rows, 128), jnp.float32),
            pltpu.VMEM((slots, 2, 2, rows), jnp.float32),
            pltpu.VMEM((slots, 2, 2, rows), jnp.float32),
            pltpu.VMEM((n_row, 2, rows), jnp.float32),
            pltpu.VMEM((n_row, 2, rows), jnp.float32),
            dma((n_row, CHUNKS)),
            dma((slots, 2, PARTS)),
            dma((n_row,)),
            dma((slots, 2)),
            dma((CHUNKS * n_row,)),
            dma((slots, PARTS)),
            dma((slots, PARTS)),
            dma((2, PARTS)),
            dma((n_row,)),
            dma((slots, 2)),
        ],
        compiler_params=pltpu.CompilerParams(
            collective_id=0, has_side_effects=True, vmem_limit_bytes=55900000
        ),
        cost_estimate=pl.CostEstimate(
            flops=2 * rows * 2 * rows * n_row * seg_len * slots,
            bytes_accessed=rows * seg_len * 4,
            transcendentals=0,
        ),
    )(segments, exclusion)


def solution(mesh):
    return jax.shard_map(
        shards,
        mesh=mesh,
        in_specs=(P(("row", "col"), None), P()),
        out_specs=P(None, ("row", "col")),
        check_vma=False,
    )
```

time: 35.1 us -> 32.2 us (0.917)
  Pallas kernels: 33.8 us -> 30.8 us
    pallas_call x1, Pallas kernels: 33.8 us -> 30.8 us  [shards(): pl.pallas_call(functools.partial(kernel, n_row, n_col), out_shape=jax.Sha...]
where the time goes in v6:
time: 32.2 us; the launch traced here: 32 us
  Pallas kernels  30.8 us (96%)
  between operations  0.66 us (2%)
  local copies, waits for them, and re-layouts  0.58 us (2%)
    pallas_call x1, Pallas kernels, shards(): pl.pallas_call(functools.partial(kernel, n_row, n_col), out_shape=jax.Sha...  30.8 us

profile of v6, /device:TPU:0, one launch (start us, length us, event | category | flops | bytes accessed | tf_op | source)
XLA Modules:
  0.0 32.0 jit_solution(2137221935698080986)
XLA Ops:
  0.7 30.8 %shard_map.28 = f32[2,384]{1,0:T(2,128)S(1)} custom-call(f32[384,512]{1,0:T(8,128)} %seg_hbm.1, s32[1]{0:T(128)S(6)} %copy.4.exclusion_ref), custom_call_target="tpu_custom_call" | custom-call | flops 3623878656 | bytes 786432 | tf_op jit(solution)/shard_map/pallas_call | solution.py:439
  31.4 0.6 %copy.5 = f32[2,384]{1,0:T(2,128)} copy(f32[2,384]{1,0:T(2,128)S(1)} %shard_map.28) | data formatting | bytes 6144

commit v7 on v6

--- a/solution.py
+++ b/solution.py
@@ -43,7 +43,7 @@
     tie_recv = (my_z % max(tie, 1) + upper) % 2 == 1
     tie_send = (my_z % max(tie, 1) + upper) % 2 == 0
     forwarding = n_row == 4
-    passing = n_z == 4
+    passing = False
     passes = my_z == 1
     if forwarding:
         x_peer = my_l + 1 - 2 * (my_l % 2)

time: 32.2 us -> 32.4 us (level)
  no operation moved by 1% of the time
where the time goes in v7:
time: 32.4 us; the launch traced here: 32.3 us
  Pallas kernels  31 us (96%)
  between operations  0.66 us (2%)
  local copies, waits for them, and re-layouts  0.58 us (2%)
    pallas_call x1, Pallas kernels, shards(): pl.pallas_call(functools.partial(kernel, n_row, n_col), out_shape=jax.Sha...  31 us

profile of v7, /device:TPU:0, one launch (start us, length us, event | category | flops | bytes accessed | tf_op | source)
XLA Modules:
  0.0 32.3 jit_solution(2448751436697258511)
XLA Ops:
  0.7 31.0 %shard_map.28 = f32[2,384]{1,0:T(2,128)S(1)} custom-call(f32[384,512]{1,0:T(8,128)} %seg_hbm.1, s32[1]{0:T(128)S(6)} %copy.4.exclusion_ref), custom_call_target="tpu_custom_call" | custom-call | flops 3623878656 | bytes 786432 | tf_op jit(solution)/shard_map/pallas_call | solution.py:439
  31.7 0.6 %copy.5 = f32[2,384]{1,0:T(2,128)} copy(f32[2,384]{1,0:T(2,128)S(1)} %shard_map.28) | data formatting | bytes 6144

commit v8 on v7

--- a/solution.py
+++ b/solution.py
@@ -10,7 +10,7 @@
 
 MESH = pl.DeviceIdType.MESH
 NONE = -3.0
-CHUNKS = 4
+CHUNKS = 2
 PARTS = 3
 TILE = 256
 

time: 32.4 us -> 33.9 us (1.046)
  Pallas kernels: 31 us -> 32.5 us
    pallas_call x1, Pallas kernels: 31 us -> 32.5 us  [shards(): pl.pallas_call(functools.partial(kernel, n_row, n_col), out_shape=jax.Sha...]
where the time goes in v8:
time: 33.9 us; the launch traced here: 33.7 us
  Pallas kernels  32.5 us (96%)
  between operations  0.66 us (2%)
  local copies, waits for them, and re-layouts  0.58 us (2%)
    pallas_call x1, Pallas kernels, shards(): pl.pallas_call(functools.partial(kernel, n_row, n_col), out_shape=jax.Sha...  32.5 us

profile of v8, /device:TPU:0, one launch (start us, length us, event | category | flops | bytes accessed | tf_op | source)
XLA Modules:
  0.0 33.7 jit_solution(15227740713034931699)
XLA Ops:
  0.7 32.5 %shard_map.28 = f32[2,384]{1,0:T(2,128)S(1)} custom-call(f32[384,512]{1,0:T(8,128)} %seg_hbm.1, s32[1]{0:T(128)S(6)} %copy.4.exclusion_ref), custom_call_target="tpu_custom_call" | custom-call | flops 3623878656 | bytes 786432 | tf_op jit(solution)/shard_map/pallas_call | solution.py:439
  33.1 0.6 %copy.5 = f32[2,384]{1,0:T(2,128)} copy(f32[2,384]{1,0:T(2,128)S(1)} %shard_map.28) | data formatting | bytes 6144
